TPU v7x, 256 devices: a whole 4x4x8 slice. The times are simulated.
256 devices in a mesh: rows: 32 (over x, z), ch: 8 (over y, core).
Axes of the slice: x: 4, y: 4, z: 8, core: 2. Of those that a mesh axis runs over, the one named last changes fastest.
Arguments:
- inputs: bfloat16 [1, 512, 256, 256], P(None, 'rows', 'ch'), may hold values from -44 to 44
- w_expand: bfloat16 [256, 1536], P(None, 'ch'), may hold values from -0.375 to 0.375
- kernel: bfloat16 [9, 1536], P(None, 'ch'), may hold values from -2.390625 to 2.390625
- w_se1: bfloat16 [1536, 64], P('ch'), may hold values from -0.4375 to 0.4375
- w_se2: bfloat16 [64, 1536], P(None, 'ch'), may hold values from -1.5 to 1.5
- w_project: bfloat16 [1536, 256], P('ch'), may hold values from -0.4375 to 0.4375
- cotangent: bfloat16 [1, 512, 256, 256], P(None, 'rows', 'ch'), may hold values from -6 to 6
Outputs:
- output: bfloat16 [1, 512, 256, 256], P(None, 'rows', 'ch')
- d_input: bfloat16 [1, 512, 256, 256], P(None, 'rows', 'ch')
- d_w_expand: float32 [256, 1536], P(None, 'ch')
- d_kernel: float32 [9, 1536], P(None, 'ch')
- d_w_se1: float32 [1536, 64], P('ch')
- d_w_se2: float32 [64, 1536], P(None, 'ch')
- d_w_project: float32 [1536, 256], P('ch')
All inputs are finite; a program needn't handle non-finite values.
Results may differ from a plain program's by a relative error of at most 0.028.
Values may be sent and summed in bfloat16 or wider, within the bound.
A program may use at most 64 MiB of HBM per device.

v0:
```python
import math

import jax
import jax.numpy as jnp
from jax import lax
from jax.sharding import PartitionSpec as P


def extended(block, sides, width):
    for axis, dim in sides:
        count = lax.axis_size(axis)
        forward = [(i, i + 1) for i in range(count - 1)]
        backward = [(target, source) for source, target in forward]
        low = lax.ppermute(
            lax.slice_in_dim(block, block.shape[dim] - width, None, axis=dim), axis, forward
        )
        high = lax.ppermute(lax.slice_in_dim(block, 0, width, axis=dim), axis, backward)
        block = jnp.concatenate([low, block, high], axis=dim)
    return block


def silu_slope(values):
    sig = jax.nn.sigmoid(values)
    return sig * (1.0 + values * (1.0 - sig))


def depth_apply(padded, kern, height, width):
    total = jnp.zeros((height, width, padded.shape[2]), jnp.float32)
    for tap_row in range(3):
        for tap_col in range(3):
            window = padded[tap_row : tap_row + height, tap_col : tap_col + width].astype(
                jnp.float32
            )
            total = total + kern[3 * tap_row + tap_col] * window
    return total


def tap_sums(grad_depth, padded, height, width):
    grad_vals = grad_depth.astype(jnp.float32)
    parts = []
    for tap_row in range(3):
        for tap_col in range(3):
            window = padded[tap_row : tap_row + height, tap_col : tap_col + width].astype(
                jnp.float32
            )
            parts.append(jnp.sum(grad_vals * window, axis=(0, 1)))
    return jnp.stack(parts)


def per_device(inputs, w_expand, kernel, w_se1, w_se2, w_project, cotangent):
    highest = lax.Precision.HIGHEST
    rows_dev = inputs.shape[1]
    cols_dev = inputs.shape[2]
    chans = inputs.shape[3]
    se_width = w_se1.shape[1]
    map_rows = rows_dev * lax.axis_size("rows")
    map_cols = cols_dev * lax.axis_size("ch")
    area = float(map_rows * map_cols)
    grad_scale = 1.0 / math.sqrt(inputs.shape[0] * map_rows * map_cols)
    expanded_loc = w_expand.shape[1]
    kern = kernel.astype(jnp.float32)
    se_down = w_se1.astype(jnp.float32)
    se_up = w_se2.astype(jnp.float32)

    def column_step(totals, pair):
        image, grad_out = pair
        whole_in = lax.all_gather(image, "ch", axis=1, tiled=True)
        width = whole_in.shape[1]
        flat_in = whole_in.reshape(-1, chans)
        expand_pre = jnp.dot(flat_in, w_expand, preferred_element_type=jnp.float32).reshape(
            rows_dev, width, expanded_loc
        )
        act_one = jax.nn.silu(expand_pre).astype(jnp.bfloat16)
        rimmed = extended(act_one, (("rows", 0),), 1)
        padded_one = jnp.pad(rimmed, ((0, 0), (1, 1), (0, 0)))
        depth_pre = depth_apply(padded_one, kern, rows_dev, width)
        act_two = jax.nn.silu(depth_pre).astype(jnp.bfloat16)
        pooled_part = jnp.sum(act_two.astype(jnp.float32), axis=(0, 1)) / area
        pooled = lax.psum(pooled_part, "rows")
        squeeze_pre = lax.psum(jnp.dot(pooled, se_down, precision=highest), "ch")
        squeeze_act = jax.nn.silu(squeeze_pre)
        gate_vals = jax.nn.sigmoid(jnp.dot(squeeze_act, se_up, precision=highest))
        hidden = (act_two.astype(jnp.float32) * gate_vals).astype(jnp.bfloat16)
        flat_hidden = hidden.reshape(-1, expanded_loc)
        proj_part = jnp.dot(flat_hidden, w_project, preferred_element_type=jnp.float32).reshape(
            rows_dev, width, chans
        )
        projected = lax.psum_scatter(
            proj_part.astype(jnp.bfloat16), "ch", scatter_dimension=1, tiled=True
        ).astype(jnp.float32)
        output = (image.astype(jnp.float32) + projected).astype(jnp.bfloat16)
        whole_grad = lax.all_gather(grad_out, "ch", axis=1, tiled=True)
        flat_grad = whole_grad.reshape(-1, chans)
        grad_hidden = jnp.dot(flat_grad, w_project.T, preferred_element_type=jnp.float32).reshape(
            rows_dev, width, expanded_loc
        )
        grad_project = jnp.dot(flat_hidden.T, flat_grad, preferred_element_type=jnp.float32)
        grad_gate_part = jnp.sum(grad_hidden * act_two.astype(jnp.float32), axis=(0, 1))
        gate_slope = gate_vals * (1.0 - gate_vals)
        grad_excite_part = grad_gate_part * gate_slope
        grad_gate = lax.psum(grad_gate_part, "rows")
        squeeze_back = lax.psum(jnp.dot(grad_gate * gate_slope, se_up.T, precision=highest), "ch")
        grad_squeeze = squeeze_back * silu_slope(squeeze_pre)
        grad_up = jnp.outer(squeeze_act, grad_excite_part)
        grad_down = jnp.outer(pooled_part, grad_squeeze)
        grad_pooled = jnp.dot(grad_squeeze, se_down.T, precision=highest)
        grad_act_two = grad_hidden * gate_vals + grad_pooled / area
        grad_depth = (grad_act_two * silu_slope(depth_pre)).astype(jnp.bfloat16)
        grad_rim = extended(grad_depth, (("rows", 0),), 1)
        padded_grad = jnp.pad(grad_rim, ((0, 0), (1, 1), (0, 0)))
        grad_act_one = depth_apply(padded_grad, kern[::-1], rows_dev, width)
        grad_kern = tap_sums(grad_depth, padded_one, rows_dev, width)
        grad_expand_pre = (grad_act_one * silu_slope(expand_pre)).astype(jnp.bfloat16)
        flat_ge = grad_expand_pre.reshape(-1, expanded_loc)
        grad_expand = jnp.dot(flat_in.T, flat_ge, preferred_element_type=jnp.float32)
        back_part = jnp.dot(flat_ge, w_expand.T, preferred_element_type=jnp.float32).reshape(
            rows_dev, width, chans
        )
        back_in = lax.psum_scatter(
            back_part.astype(jnp.bfloat16), "ch", scatter_dimension=1, tiled=True
        ).astype(jnp.float32)
        grad_input = (grad_out.astype(jnp.float32) + back_in).astype(jnp.bfloat16)
        fresh = (grad_expand, grad_kern, grad_down, grad_up, grad_project)
        totals = tuple((old + new for old, new in zip(totals, fresh)))
        return (totals, (output, grad_input))

    init = (
        jnp.zeros((chans, expanded_loc), jnp.float32),
        jnp.zeros((9, expanded_loc), jnp.float32),
        jnp.zeros((expanded_loc, se_width), jnp.float32),
        jnp.zeros((se_width, expanded_loc), jnp.float32),
        jnp.zeros((expanded_loc, chans), jnp.float32),
    )
    totals, (output, d_input) = lax.scan(column_step, init, (inputs, cotangent))
    scaled = tuple((part * grad_scale for part in totals))
    grad_expand, grad_kern, grad_down, grad_up, grad_project = (
        lax.psum(scaled[0].astype(jnp.bfloat16), "rows").astype(jnp.float32),
        lax.psum(scaled[1].astype(jnp.bfloat16), "rows").astype(jnp.float32),
        lax.psum(scaled[2].astype(jnp.bfloat16), "rows").astype(jnp.float32),
        lax.psum(scaled[3].astype(jnp.bfloat16), "rows").astype(jnp.float32),
        lax.psum(scaled[4].astype(jnp.bfloat16), "rows").astype(jnp.float32),
    )
    return (output, d_input, grad_expand, grad_kern, grad_down, grad_up, grad_project)


def solution(mesh):
    return jax.shard_map(
        per_device,
        mesh=mesh,
        in_specs=(
            P(None, "rows", "ch", None),
            P(None, "ch"),
            P(None, "ch"),
            P("ch", None),
            P(None, "ch"),
            P("ch", None),
            P(None, "rows", "ch", None),
        ),
        out_specs=(
            P(None, "rows", "ch", None),
            P(None, "rows", "ch", None),
            P(None, "ch"),
            P(None, "ch"),
            P("ch", None),
            P(None, "ch"),
            P("ch", None),
        ),
        check_vma=False,
    )
```

profile of v0, /device:TPU:8, one launch (start us, length us, event | category | flops | bytes accessed | tf_op | source)
XLA Modules:
  0.0 420.1 jit_solution(1248599961671391541)
XLA Ops:
  7.2 0.0 copy-start
  7.2 0.0 all-gather.5.cloned.1.call-start
  7.2 0.7 all-gather.5.cloned.1.call-update
  7.9 0.0 all-gather.7.cloned.1.call-start
  8.0 0.7 all-gather.7.cloned.1.call-update
  8.7 0.0 copy-start.8
  8.7 0.0 all-reduce.7.cloned.1.call-start
  8.7 30.8 %all-gather.5.cloned.1.call-done = bf16[1,16,256,256]{3,2,1,0:T(8,128)(2,1)} async-done(((bf16[1,16,32,256]{3,2,1,0:T(8,128)(2,1)}), bf16[1,16,256,256]{3,2,1,0:T(8,128)(2,1)}) %all-gather.5.cloned.1.call-update) | async-done | bytes 2097168 | tf_op jit(solution)/shard_map/while/body/eval_jaxpr/all_gather | solution.py:67
  39.6 4.3 %multiply_convert_fusion.2 = (bf16[16,256,192]{1,2,0:T(8,128)(2,1)S(1)}, f32[16,256,192]{1,2,0:T(8,128)}) fusion(bf16[256,192]{0,1:T(8,128)(2,1)} %param.8, bf16[1,16,256,256]{3,2,1,0:T(8,128)(2,1)} %all-gather.5.cloned.1.call-done), kind=kOutput, calls=%fused_computation.54 | convolution fusion | flops 406585344 | bytes 6914048 | tf_op jit(solution)/shard_map/while/body/eval_jaxpr/dot_general | solution.py:70
  43.9 3.5 collective-permute-start
  47.4 1.3 collective-permute-start.1
  48.7 0.0 copy-done.8
  48.7 1.1 collective-permute-done
  49.8 4.1 collective-permute-done.1
  54.0 0.0 copy-done.1
  54.0 1.8 select_maximum_fusion.2
  55.8 13.7 %all-gather.7.cloned.1.call-done = bf16[1,16,256,256]{3,2,1,0:T(8,128)(2,1)} async-done(((bf16[1,16,32,256]{3,2,1,0:T(8,128)(2,1)}), bf16[1,16,256,256]{3,2,1,0:T(8,128)(2,1)}) %all-gather.7.cloned.1.call-update) | async-done | bytes 2097168 | tf_op jit(solution)/shard_map/while/body/eval_jaxpr/all_gather | solution.py:92
  69.5 0.0 copy-done
  69.5 9.7 %fusion.10 = (f32[192]{0:T(256)S(1)}, f32[192]{0:T(256)S(1)}, bf16[16,256,192]{1,2,0:T(8,128)(2,1)}, f32[16,256,192]{1,2,0:T(8,128)}, f32[16,256,192]{1,2,0:T(8,128)}) fusion(bf16[18,258,192]{1,2,0:T(8,128)(2,1)S(1)} %select_maximum_fusion.2, f32[192]{0:T(256)S(1)} %bitcast.128, bf16[1,256,192]{1,2,0:T(8,128)(2,1)S(1)} %collective-permute-done.1, ...), kind=kOutput, calls=%fused_computation.34 | convolution fusion | flops 431750784 | bytes 21274880 | tf_op jit(solution)/shard_map/while/body/eval_jaxpr/dot_general | solution.py:94
  79.2 75.1 %all-reduce.2 = (f32[192]{0:T(256)S(1)}, f32[192]{0:T(256)S(1)}) all-reduce(f32[192]{0:T(256)S(1)} %broadcast_multiply_fusion.1, f32[192]{0:T(256)S(1)} %get-tuple-element.64), channel_id=1, replica_groups=mesh['rows'=32,'ch'=8] {'rows'}, use_global_device_ids=true, to_apply=%region_1.2 | all-reduce | flops 384 | bytes 3072 | tf_op jit(solution)/shard_map/while/body/eval_jaxpr/psum | solution.py:79
  154.2 0.0 copy-done.7
  154.2 0.1 convolution_bitcast_fusion.1
  154.3 10.5 %psum.68 = f32[64]{0:T(128)S(1)} all-reduce(f32[64]{0:T(128)S(1)} %convolution_bitcast_fusion.1), channel_id=1, replica_groups=mesh['rows'=32,'ch'=8] {'ch'}, use_global_device_ids=true, to_apply=%region_2.3 | all-reduce | flops 64 | bytes 512 | tf_op jit(solution)/shard_map/while/body/eval_jaxpr/psum | solution.py:80
  164.8 0.0 copy-done.6
  164.8 0.1 fusion.73
  165.0 0.1 convolution_bitcast_fusion
  165.1 13.0 %psum.70 = f32[64]{0:T(128)S(1)} all-reduce(f32[64]{0:T(128)S(1)} %convolution_bitcast_fusion), channel_id=1, replica_groups=mesh['rows'=32,'ch'=8] {'ch'}, use_global_device_ids=true, to_apply=%region_6.7 | all-reduce | flops 64 | bytes 512 | tf_op jit(solution)/shard_map/while/body/eval_jaxpr/psum | solution.py:102
  178.1 0.1 fusion.67
  178.2 0.0 copy-start.11
  178.2 8.9 %fusion.26 = (f32[192]{0:T(256)S(1)}, f32[192]{0:T(256)S(1)}, f32[192]{0:T(256)S(1)}, f32[192]{0:T(256)S(1)}, f32[192]{0:T(256)S(1)}, /*index=5*/f32[192]{0:T(25...) fusion(bf16[18,258,192]{1,2,0:T(8,128)(2,1)S(1)} %select_maximum_fusion.2, ...), kind=kLoop, calls=%fused_computation.50 | loop fusion | flops 32241984 | bytes 19079424 | tf_op jit(solution)/shard_map/while/body/eval_jaxpr/reduce_sum | solution.py:46
  187.2 1.3 collective-permute-start.2
  188.5 1.3 collective-permute-start.3
  189.8 0.0 copy-done.10
  189.8 0.0 copy-done.11
  189.8 1.3 fusion.48
  191.1 0.0 collective-permute-done.2
  191.1 3.9 collective-permute-done.3
  195.0 1.8 select_maximum_fusion
  196.8 0.0 copy-done.2
  196.8 5.3 %fusion.17 = bf16[16,256,192]{1,2,0:T(8,128)(2,1)S(1)} fusion(bf16[16,256,192]{1,2,0:T(8,128)(2,1)S(1)} %get-tuple-element.75, f32[16,256,192]{1,2,0:T(8,128)S(1)} %copy-done.2, bf16[18,258,192]{1,2,0:T(8,128)(2,1)S(1)} %select_maximum_fusion, bf16[1,256,192]{1,2,0:T(8,128)(2,1)S(1)} %collective-permute-done.3, ...), kind=kLoop, calls=%fused_computation.41 | loop fusion | flops 29097984 | bytes 15932160 | tf_op jit(solution)/shard_map/while/body/eval_jaxpr/convert_element_type | solution.py:113
  202.1 1.2 fusion.54
  203.4 0.0 all-reduce.7.cloned.1.call-update
  203.4 0.0 copy-start.5
  203.4 0.0 reduce-scatter.3.cloned.1.call-start
  203.5 3.6 convolution_convert_fusion.1
  207.1 0.0 reduce-scatter.3.cloned.1.call-update
  207.1 0.0 copy-start.3
  207.1 0.0 copy-start.4
  207.1 0.0 reduce-scatter.5.cloned.1.call-start
  207.2 2.1 convolution_convert_fusion
  209.3 0.0 reduce-scatter.5.cloned.1.call-update
  209.3 0.1 multiply_convert_fusion.4
  209.4 0.1 multiply_convert_fusion.3
  209.5 137.9 %all-reduce.3 = (bf16[9,192]{1,0:T(8,128)(2,1)S(1)}, bf16[192,64]{0,1:T(8,128)(2,1)S(1)}, bf16[64,192]{1,0:T(8,128)(2,1)S(1)}) all-reduce(bf16[9,192]{1,0:T(8,128)(2,1)S(1)} %multiply_convert_fusion.5, bf16[192,64]{0,1:T(8,128)(2,1)S(1)} %multiply_convert_fusion.4, ...), channel_id=1, replica_groups=mesh['rows'=32,'ch'=8] {'rows'}, use_global_device_ids=true, to_apply=%region_18.19 | all-reduce | flops 26304 | bytes 105216 | tf_op jit(solution)/shard_map/psum | solution.py:138
  347.4 0.6 convert_element_type.220
  348.0 0.6 convert_element_type.222
  348.7 0.6 convert_element_type.224
  349.3 1.6 convert_element_type.218
  350.9 1.6 convert_element_type.226
  352.5 21.8 %reduce-scatter.3.cloned.1.call-done = bf16[16,32,256]{2,1,0:T(8,128)(2,1)} async-done(((bf16[16,256,256]{2,1,0:T(8,128)(2,1)}), bf16[16,32,256]{2,1,0:T(8,128)(2,1)}) %reduce-scatter.3.cloned.1.call-update) | async-done | bytes 262160 | tf_op jit(solution)/shard_map/while/body/eval_jaxpr/reduce_scatter | solution.py:88
  374.2 1.7 fusion.61
  376.0 35.9 %reduce-scatter.5.cloned.1.call-done = bf16[16,32,256]{2,1,0:T(8,128)(2,1)} async-done(((bf16[16,256,256]{2,1,0:T(8,128)(2,1)}), bf16[16,32,256]{2,1,0:T(8,128)(2,1)}) %reduce-scatter.5.cloned.1.call-update) | async-done | bytes 262160 | tf_op jit(solution)/shard_map/while/body/eval_jaxpr/reduce_scatter | solution.py:119
  411.9 0.0 copy-done.4
  411.9 1.7 fusion.62
  (21 shorter events, 0.2 us)
Async XLA Ops:
  7.2 62.3 %copy-start = (bf16[192,256]{1,0:T(8,128)(2,1)S(1)}, bf16[192,256]{1,0:T(8,128)(2,1)}, u32[]{:S(2)}) copy-start(bf16[192,256]{1,0:T(8,128)(2,1)} %param.12) | copy-start | bytes 294916
  7.2 32.4 %all-gather.5.cloned.1.call-start = ((), (), s32[]{:S(2)}) async-start(), calls=%async_computation.4 | async-start | bytes 2359296 | tf_op jit(solution)/shard_map/while/body/eval_jaxpr/all_gather | solution.py:67
  7.9 61.6 %all-gather.7.cloned.1.call-start = ((), (), s32[]{:S(2)}) async-start(), calls=%async_computation.5 | async-start | bytes 2359296 | tf_op jit(solution)/shard_map/while/body/eval_jaxpr/all_gather | solution.py:92
  8.7 40.0 %copy-start.8 = (bf16[9,192]{1,0:T(8,128)(2,1)S(1)}, bf16[9,192]{1,0:T(8,128)(2,1)}, u32[]{:S(2)}) copy-start(bf16[9,192]{1,0:T(8,128)(2,1)} %param.9) | copy-start | bytes 10372
  8.7 340.6 %all-reduce.7.cloned.1.call-start = ((), (), s32[]{:S(2)}) async-start(), calls=%async_computation.6 | async-start | bytes 393216 | tf_op jit(solution)/shard_map/psum | solution.py:137
  43.9 10.1 %copy-start.1 = (bf16[16,256,192]{1,2,0:T(8,128)(2,1)}, bf16[16,256,192]{1,2,0:T(8,128)(2,1)S(1)}, u32[]{:S(2)}) copy-start(bf16[16,256,192]{1,2,0:T(8,128)(2,1)S(1)} %get-tuple-element.93) | copy-start | bytes 4718596
  43.9 5.9 %collective-permute-start = (bf16[1,256,192]{1,2,0:T(8,128)(2,1)S(1)}, bf16[1,256,192]{1,2,0:T(8,128)(2,1)S(1)}, u32[]{:S(2)}, u32[]{:S(2)}) collective-permute-start(bf16[1,256,192]{1,2,0:T(8,128)(2,1)S(1)} %get-tuple-element.82), channel_id=1, source_target_pairs={{0,8},{8,16},{16,24},{24,32},{32,40},{40,48},{48,56},{56,64},{64,7... | collective-permute-start | bytes 294920 | tf_op jit(solution)/shard_map/while/body/eval_jaxpr/ppermute | solution.py:14
  47.4 6.6 %collective-permute-start.1 = (bf16[1,256,192]{1,2,0:T(8,128)(2,1)S(1)}, bf16[1,256,192]{1,2,0:T(8,128)(2,1)S(1)}, u32[]{:S(2)}, u32[]{:S(2)}) collective-permute-start(bf16[1,256,192]{1,2,0:T(8,128)(2,1)S(1)} %get-tuple-element.83), channel_id=1, source_target_pairs={{8,0},{16,8},{24,16},{32,24},{40,32},{48,40},{56,48},{64,56},{72,6... | collective-permute-start | bytes 294920 | tf_op jit(solution)/shard_map/while/body/eval_jaxpr/ppermute | solution.py:17
  69.5 84.8 %copy-start.7 = (bf16[192,64]{0,1:T(8,128)(2,1)S(1)}, bf16[192,64]{0,1:T(8,128)(2,1)}, u32[]{:S(2)}) copy-start(bf16[192,64]{0,1:T(8,128)(2,1)} %param.10) | copy-start | bytes 73732
  69.5 95.3 %copy-start.6 = (bf16[64,192]{1,0:T(8,128)(2,1)S(1)}, bf16[64,192]{1,0:T(8,128)(2,1)}, u32[]{:S(2)}) copy-start(bf16[64,192]{1,0:T(8,128)(2,1)} %param.11) | copy-start | bytes 73732
  178.2 11.6 %copy-start.10 = (bf16[1,16,256,256]{3,2,1,0:T(8,128)(2,1)S(1)}, bf16[1,16,256,256]{3,2,1,0:T(8,128)(2,1)}, u32[]{:S(2)}) copy-start(bf16[1,16,256,256]{3,2,1,0:T(8,128)(2,1)} %all-gather.7.cloned.1.call-done) | copy-start | bytes 6291460
  178.2 11.6 %copy-start.11 = (bf16[16,256,192]{1,2,0:T(8,128)(2,1)S(1)}, bf16[16,256,192]{1,2,0:T(8,128)(2,1)}, u32[]{:S(2)}) copy-start(bf16[16,256,192]{1,2,0:T(8,128)(2,1)} %get-tuple-element.78) | copy-start | bytes 4718596
  187.2 3.9 collective-permute-start.2
  188.5 6.5 %collective-permute-start.3 = (bf16[1,256,192]{1,2,0:T(8,128)(2,1)S(1)}, bf16[1,256,192]{1,2,0:T(8,128)(2,1)S(1)}, u32[]{:S(2)}, u32[]{:S(2)}) collective-permute-start(bf16[1,256,192]{1,2,0:T(8,128)(2,1)S(1)} %get-tuple-element.81), channel_id=1, source_target_pairs={{8,0},{16,8},{24,16},{32,24},{40,32},{48,40},{56,48},{64,56},{72,6... | collective-permute-start | bytes 294920 | tf_op jit(solution)/shard_map/while/body/eval_jaxpr/ppermute | solution.py:17
  191.1 5.7 %copy-start.2 = (f32[16,256,192]{1,2,0:T(8,128)S(1)}, f32[16,256,192]{1,2,0:T(8,128)}, u32[]{:S(2)}) copy-start(f32[16,256,192]{1,2,0:T(8,128)} %get-tuple-element.94) | copy-start | bytes 9437188
  196.8 5.3 %copy-start.9 = (bf16[1,16,256,256]{3,2,1,0:T(8,128)(2,1)S(1)}, bf16[1,16,256,256]{3,2,1,0:T(8,128)(2,1)}, u32[]{:S(2)}) copy-start(bf16[1,16,256,256]{3,2,1,0:T(8,128)(2,1)} %all-gather.5.cloned.1.call-done) | copy-start | bytes 6291460
  203.4 3.8 copy-start.5
  203.4 170.8 %reduce-scatter.3.cloned.1.call-start = ((), (), s32[]{:S(2)}) async-start(), calls=%async_computation.2 | async-start | bytes 2359296 | tf_op jit(solution)/shard_map/while/body/eval_jaxpr/reduce_scatter | solution.py:88
  207.1 167.1 %copy-start.3 = (bf16[1,16,32,256]{3,2,1,0:T(8,128)(2,1)S(1)}, bf16[1,16,32,256]{3,2,1,0:T(8,128)(2,1)}, u32[]{:S(2)}) copy-start(bf16[1,16,32,256]{3,2,1,0:T(8,128)(2,1)} %param.7) | copy-start | bytes 786436
  207.1 204.8 %copy-start.4 = (bf16[1,16,32,256]{3,2,1,0:T(8,128)(2,1)S(1)}, bf16[1,16,32,256]{3,2,1,0:T(8,128)(2,1)}, u32[]{:S(2)}) copy-start(bf16[1,16,32,256]{3,2,1,0:T(8,128)(2,1)} %param.13) | copy-start | bytes 786436
  207.1 204.7 %reduce-scatter.5.cloned.1.call-start = ((), (), s32[]{:S(2)}) async-start(), calls=%async_computation.3 | async-start | bytes 2359296 | tf_op jit(solution)/shard_map/while/body/eval_jaxpr/reduce_scatter | solution.py:119
Sparse Core Ops, SparseCore 0:
  9.9 29.6 all-gather.4
  41.4 28.0 all-gather.6
  203.5 137.6 all-reduce.6
  343.8 30.3 reduce-scatter.2
  376.8 35.0 reduce-scatter.4
where the time goes:
time: 424 us; the launch traced here: 420 us
  blocking collectives  236 us (56%)
  waiting for transfers between devices  113 us (27%)
  other arithmetic  26.6 us (6%)
  matrix products  22.7 us (5%)
  between operations  14 us (3%)
  starting transfers between devices  7.54 us (2%)
    psum x1, blocking collectives, per_device(): lax.psum(scaled[1].astype(jnp.bfloat16), 'rows').astype(jnp.float32)  138 us
    psum x1, blocking collectives, column_step(): pooled = lax.psum(pooled_part, 'rows')  75.1 us
    reduce_scatter x1, waiting for transfers between devices, column_step(): lax.psum_scatter(back_part.astype(jnp.bfloat16), 'ch', scatter_dimension=...  35.9 us
    all_gather x1, waiting for transfers between devices, column_step(): whole_in = lax.all_gather(image, 'ch', axis=1, tiled=True)  30.8 us
    reduce_scatter x1, waiting for transfers between devices, column_step(): lax.psum_scatter(proj_part.astype(jnp.bfloat16), 'ch', scatter_dimension=...  21.8 us
    all_gather x1, waiting for transfers between devices, column_step(): whole_grad = lax.all_gather(grad_out, 'ch', axis=1, tiled=True)  13.7 us
    psum x1, blocking collectives, column_step(): lax.psum(jnp.dot(grad_gate * gate_slope, se_up.T, precision=highest), 'ch')  13 us
    psum x1, blocking collectives, column_step(): squeeze_pre = lax.psum(jnp.dot(pooled, se_down, precision=highest), 'ch')  10.5 us
  transfers between devices with their start and end apart: 9, of which 7 were waited for; matrix products, arithmetic and copies ran while one was open for 5% of the time, Pallas kernels for 0%

commit v1 on v0

v1 whole, which is shorter than its diff:
```python
import functools
import math

import jax
import jax.numpy as jnp
from jax import lax
from jax.experimental import pallas as pl
from jax.experimental.pallas import tpu as pltpu
from jax.sharding import PartitionSpec as P

MESH = pl.DeviceIdType.MESH
F32 = jnp.float32
BF16 = jnp.bfloat16

CHIPS_Z = 8
H = 16
W = 32
C = 256
S = 192
PW = 72
NT_DIMS = (((1,), (1,)), ((), ()))
TN_DIMS = (((0,), (0,)), ((), ()))


def split3(row):
    hi = row.astype(BF16).astype(F32)
    mid = (row - hi).astype(BF16).astype(F32)
    low = row - hi - mid
    rest = jnp.zeros((5, row.shape[1]), F32)
    return jnp.concatenate([hi, mid, low, rest], axis=0).astype(BF16)


def sigm(v):
    return 0.5 * jnp.tanh(0.5 * v) + 0.5


def fused(rows_n, ch_n, x_ref, c_ref, w_ref, se_ref, tap_ref,
          out_ref, din_ref, dwe_ref, dwp_ref, dk_ref, vec_ref,
          xsib, csib, rowsend, rowbuf, colsend, colbuf, wbuf, sebuf, tapbuf,
          xf, cf, xs, cs, xnat, cnat, a1, s1, gh, s2, act2, ge, ktile, gacc, dkacc,
          vbuf, zv, xv, cv, gs, ysend, yrecv, zsend, zrecv, xrecv, fsend, frecv,
          dksend, dkyr, dkzr, dkxs, dkxr, dkzs, posend, porecv,
          sib_s, sib_r, row_s, row_r, col_s, col_r, w_s, w_r, se_s, se_r, tap_s, tap_r,
          vz_s, vz_r, vx_s, vx_r, vc_s, vc_r, gy_s, gy_r, gz_s, gz_r, gx_s, gx_r, gf_s, gf_r,
          ky_s, ky_r, kz_s, kz_r, kx_s, kx_r, po_s, po_r):
    zn = CHIPS_Z if rows_n % CHIPS_Z == 0 else 2
    xn = rows_n // zn
    yn = ch_n // 2
    ce = S * yn
    nt = ce // 128
    pairs = yn // 2
    zr = S // (zn // 2)
    row = lax.axis_index("rows")
    ch = lax.axis_index("ch")
    mx, mz = row // zn, lax.rem(row, zn)
    my, mc = ch // 2, lax.rem(ch, 2)
    oc = 1 - mc

    def dev_row(step):
        return lax.rem(row + step + rows_n, rows_n)

    def dev_y(step):
        return lax.rem(my + step + yn, yn)

    def copy(src, dst, ssem, rsem, where):
        return pltpu.make_async_remote_copy(
            src_ref=src, dst_ref=dst, send_sem=ssem, recv_sem=rsem, device_id=where, device_id_type=MESH)

    def at_y(peer):
        return (row, peer * 2 + mc)

    def at_z(peer):
        return (mx * zn + peer, ch)

    def at_x(peer):
        return (peer * zn + mz, ch)

    def at_ch(peer):
        return (row, peer)

    def spread(n, me, at, src, land, ssem, rsem):
        for step in range(1, n):
            peer = lax.rem(me + step, n)
            copy(src(peer), land.at[me], ssem.at[step - 1], rsem.at[me], at(peer)).start()

    def gathered(n, me, at, src, land, ssem, rsem):
        for step in range(1, n):
            peer = lax.rem(me + step, n)
            copy(src(peer), land.at[peer], ssem.at[step - 1], rsem.at[peer], at(peer)).wait()

    barrier = pltpu.get_barrier_semaphore()
    partners = [at_ch(lax.rem(ch + s, ch_n)) for s in range(1, ch_n)]
    partners += [at_z(lax.rem(mz + s, zn)) for s in range(1, zn)]
    partners += [at_x(lax.rem(mx + s, xn)) for s in range(1, xn)]
    partners += [(dev_row(dr), my * 2 + core) for dr in (-1, 1) for core in (0, 1)]
    partners += [(dev_row(dr), dev_y(dy) * 2 + core) for dr in (-1, 0, 1) for dy in (-1, 1) for core in (0, 1)]
    for where in partners:
        pl.semaphore_signal(barrier, inc=1, device_id=where, device_id_type=MESH)

    for d, (lo, edge) in enumerate(((0, 0), (H - 2, H - 1))):
        rowsend[d, 0:2 * W] = x_ref[lo:lo + 2].reshape(2 * W, C)
        rowsend[d, 2 * W:3 * W] = c_ref[edge]
    first = mc * (W - 2)
    ri = lax.broadcasted_iota(jnp.int32, (2 * H, H * W), 0)
    ci = lax.broadcasted_iota(jnp.int32, (2 * H, H * W), 1)
    pick = (ci == (ri & (H - 1)) * W + first + (ri >> 4)).astype(F32).astype(BF16)
    colsend[0:2 * H] = jnp.dot(pick, x_ref[...].reshape(H * W, C), preferred_element_type=F32).astype(BF16)
    ri = lax.broadcasted_iota(jnp.int32, (H, H * W), 0)
    ci = lax.broadcasted_iota(jnp.int32, (H, H * W), 1)
    pick = (ci == ri * W + mc * (W - 1)).astype(F32).astype(BF16)
    colsend[2 * H:3 * H] = jnp.dot(pick, c_ref[...].reshape(H * W, C), preferred_element_type=F32).astype(BF16)

    pl.semaphore_wait(barrier, len(partners))

    sib = (row, my * 2 + oc)
    sib_copies = [copy(x_ref, xsib, sib_s.at[0], sib_r.at[0], sib), copy(c_ref, csib, sib_s.at[1], sib_r.at[1], sib)]
    row_copies = []
    for d, dr in ((0, -1), (1, 1)):
        for core in (0, 1):
            row_copies.append((copy(rowsend.at[d], rowbuf.at[1 - d, mc], row_s.at[d, core], row_r.at[1 - d, mc],
                                    (dev_row(dr), my * 2 + core)),
                               copy(rowsend.at[d], rowbuf.at[1 - d, core], row_s.at[d, core], row_r.at[1 - d, core],
                                    (dev_row(dr), my * 2 + core))))
    col_copies = []
    side = 1 - mc
    for i, dr in enumerate((-1, 0, 1)):
        for core in (0, 1):
            where = (dev_row(dr), dev_y(2 * mc - 1) * 2 + core)
            col_copies.append((copy(colsend, colbuf.at[side, 2 - i], col_s.at[i, core], col_r.at[side, 2 - i], where),
                               copy(colsend, colbuf.at[core, i], col_s.at[i, core], col_r.at[core, i], where)))
    for sent in sib_copies:
        sent.start()
    for sent, _ in row_copies + col_copies:
        sent.start()
    spread(yn, my, at_y, lambda p: tap_ref, tapbuf, tap_s, tap_r)
    spread(yn, my, at_y, lambda p: w_ref, wbuf, w_s, w_r)
    spread(ch_n, ch, at_ch, lambda p: se_ref, sebuf, se_s, se_r)

    wbuf[my] = w_ref[...]
    tapbuf[my] = tap_ref[...]
    sebuf[ch] = se_ref[...]
    mine = pl.ds(pl.multiple_of(mc * W, W), W)
    other = pl.ds(pl.multiple_of(oc * W, W), W)
    xf[2:2 + H, mine] = x_ref[...].astype(F32)
    cf[1:1 + H, mine] = c_ref[...].astype(F32)
    xnat[:, mine] = x_ref[...]
    cnat[:, mine] = c_ref[...]
    for sent in sib_copies:
        sent.wait()
    xf[2:2 + H, other] = xsib[...].astype(F32)
    cf[1:1 + H, other] = csib[...].astype(F32)
    xnat[:, other] = xsib[...]
    cnat[:, other] = csib[...]
    for _, landed in row_copies + col_copies:
        landed.wait()

    top_ok = row > 0
    low_ok = row < rows_n - 1
    left_ok = my > 0
    right_ok = my < yn - 1
    for d, ok in ((0, top_ok), (1, low_ok)):
        for core in (0, 1):
            part = rowbuf[d, core].astype(F32) * jnp.where(ok, 1.0, 0.0)
            xf[(2 + H) * d:(2 + H) * d + 2, W * core:W * core + W] = part[0:2 * W].reshape(2, W, C)
            cf[(1 + H) * d, W * core:W * core + W] = part[2 * W:3 * W]
    cols = colbuf[...].reshape(2 * 3 * 48, C)

    def rim(height, above, left_slot, right_slot):
        shape = (height * 8, 288)
        out_row = lax.broadcasted_iota(jnp.int32, shape, 0)
        src = lax.broadcasted_iota(jnp.int32, shape, 1)
        place = out_row & 7
        at_row = (out_row >> 3) - above
        third = jnp.where(at_row < 0, 0, jnp.where(at_row < H, 1, 2))
        ok = jnp.where(at_row < 0, top_ok.astype(jnp.int32), jnp.where(at_row < H, 1, low_ok.astype(jnp.int32)))
        want = third * 48 + (at_row & (H - 1))
        right_of = jnp.where(place < 4, 1, 0)
        slot = jnp.where(place < 4, right_slot(place), left_slot(place))
        ok = ok * jnp.where(slot < 0, 0, 1) * jnp.where(place < 4, right_ok.astype(jnp.int32), left_ok.astype(jnp.int32))
        want = want + right_of * 144 + slot * 16
        hit = jnp.where(src == want, ok, 0).astype(F32).astype(BF16)
        return jnp.dot(hit, cols, preferred_element_type=F32).reshape(height, 8, C)

    xf[:, 64:72] = rim(H + 4, 2, lambda k: jnp.where(k >= 6, k - 6, -1), lambda k: jnp.where(k < 2, k, -1))
    cf[:, 64:72] = rim(H + 2, 1, lambda k: jnp.where(k == 7, 2, -1), lambda k: jnp.where(k == 0, 2, -1))

    @pl.loop(0, (H + 4) // 2)
    def _(i):
        at = pl.ds(pl.multiple_of(i * 2 * PW, 2 * PW), 2 * PW)
        xs[at] = xf[pl.ds(i * 2, 2)].reshape(2 * PW, C).astype(BF16)

    @pl.loop(0, (H + 2) // 2)
    def _(i):
        at = pl.ds(pl.multiple_of(i * 2 * PW, 2 * PW), 2 * PW)
        cs[at] = cf[pl.ds(i * 2, 2)].reshape(2 * PW, C).astype(BF16)

    gathered(yn, my, at_y, lambda p: tap_ref, tapbuf, tap_s, tap_r)
    wide = jnp.concatenate([tapbuf[q].astype(F32)[:, 0:S] for q in range(yn)], axis=1)
    for t in range(nt):
        ktile[t] = wide[:, 128 * t:128 * t + 128]
    gathered(yn, my, at_y, lambda p: w_ref, wbuf, w_s, w_r)

    for b in range(pairs):
        pair = lax.rem(my // 2 + b, pairs)
        w_exp = wbuf[pl.ds(pair * 2, 2), 0].reshape(2 * S, C)
        w_pro = wbuf[pl.ds(pair * 2, 2), 1].reshape(2 * S, C)

        @pl.loop(0, (H + 4) // 2)
        def _(i):
            at = pl.ds(pl.multiple_of(i * 2 * PW, 2 * PW), 2 * PW)
            pre = lax.dot_general(xs[at], w_exp, NT_DIMS, preferred_element_type=F32)
            sig = sigm(pre)
            act = pre * sig
            slope = sig * (1.0 + (pre - act))
            for t in range(3):
                a1[pair * 3 + t, pl.ds(i * 2, 2)] = act[:, 128 * t:128 * t + 128].reshape(2, PW, 128)
                s1[pair * 3 + t, pl.ds(i * 2, 2)] = slope[:, 128 * t:128 * t + 128].reshape(2, PW, 128)

        @pl.loop(0, (H + 2) // 2)
        def _(i):
            at = pl.ds(pl.multiple_of(i * 2 * PW, 2 * PW), 2 * PW)
            back = lax.dot_general(cs[at], w_pro, NT_DIMS, preferred_element_type=F32)
            for t in range(3):
                gh[pair * 3 + t, pl.ds(i * 2, 2)] = back[:, 128 * t:128 * t + 128].reshape(2, PW, 128)

        @pl.loop(0, 3)
        def _(t3):
            t = pair * 3 + t3
            lanes = pl.ds(pl.multiple_of(t * 128, 128), 128)
            taps = [ktile[t, k:k + 1] for k in range(9)]

            def one_row(i):
                rows = [a1[t, i + r] for r in range(3)]
                parts = [taps[c] * rows[0] + taps[3 + c] * rows[1] + taps[6 + c] * rows[2] for c in range(3)]
                pre = parts[1] + pltpu.roll(parts[0], 1, 0) + pltpu.roll(parts[2], PW - 1, 0)
                sig = sigm(pre)
                act = pre * sig
                s2[t, i] = sig * (1.0 + (pre - act))
                return act[0:64]

            def center(i, sums):
                pool, gate_sum = sums
                act = one_row(i)
                act2[i - 1, :, lanes] = act.astype(BF16)
                pool = pool + jnp.sum(act.reshape(8, 8, 128), axis=0)
                gate_sum = gate_sum + jnp.sum((act * gh[t, i, 0:64]).reshape(8, 8, 128), axis=0)
                return pool, gate_sum

            one_row(0)
            one_row(H + 1)
            zero = jnp.zeros((8, 128), F32)
            pool, gate_sum = lax.fori_loop(1, H + 1, center, (zero, zero))
            vbuf[pl.ds(t, 1)] = jnp.sum(pool, axis=0, keepdims=True)
            vbuf[pl.ds(8 + t, 1)] = jnp.sum(gate_sum, axis=0, keepdims=True)

    for t in range(nt, 8):
        vbuf[t:t + 1] = jnp.zeros((1, 128), F32)
        vbuf[8 + t:9 + t] = jnp.zeros((1, 128), F32)

    spread(zn, mz, at_z, lambda p: vbuf, zv, vz_s, vz_r)
    zv[mz] = vbuf[...]

    def send_rows(g, value):
        ysend[g] = value.reshape(yn, S, C).astype(BF16)
        spread(yn, my, at_y, lambda p: ysend.at[g, p], yrecv.at[g], gy_s.at[g], gy_r.at[g])
        yrecv[g, my] = ysend[g, my]

    def send_z(g):
        gathered(yn, my, at_y, lambda p: ysend.at[g, p], yrecv.at[g], gy_s.at[g], gy_r.at[g])
        total = yrecv[g, 0].astype(F32)
        for q in range(1, yn):
            total = total + yrecv[g, q].astype(F32)
        for q in range(zn):
            zsend[g, q] = total[zr * (q // 2):zr * (q // 2) + zr, 128 * (q % 2):128 * (q % 2) + 128].astype(BF16)
        spread(zn, mz, at_z, lambda p: zsend.at[g, p], zrecv.at[g], gz_s.at[g], gz_r.at[g])
        zrecv[g, mz] = zsend[g, mz]

    def send_x(g):
        gathered(zn, mz, at_z, lambda p: zsend.at[g, p], zrecv.at[g], gz_s.at[g], gz_r.at[g])
        total = zrecv[g, 0].astype(F32)
        for q in range(1, zn):
            total = total + zrecv[g, q].astype(F32)
        fsend[g, 0] = total.astype(BF16)
        spread(xn, mx, at_x, lambda p: fsend.at[g, 0], xrecv.at[g], gx_s.at[g], gx_r.at[g])
        xrecv[g, mx] = fsend[g, 0]

    def send_back(g):
        gathered(xn, mx, at_x, lambda p: fsend.at[g, 0], xrecv.at[g], gx_s.at[g], gx_r.at[g])
        total = xrecv[g, 0].astype(F32)
        for q in range(1, xn):
            total = total + xrecv[g, q].astype(F32)
        fsend[g, 1] = total.astype(BF16)
        spread(zn, mz, at_z, lambda p: fsend.at[g, 1], frecv.at[g], gf_s.at[g], gf_r.at[g])
        frecv[g, mz] = fsend[g, 1]

    def whole(g, into):
        gathered(zn, mz, at_z, lambda p: fsend.at[g, 1], frecv.at[g], gf_s.at[g], gf_r.at[g])
        for q in range(zn):
            into[zr * (q // 2):zr * (q // 2) + zr, 128 * (q % 2):128 * (q % 2) + 128] = frecv[g, q].astype(F32)

    cot_flat = cnat[...].reshape(H * 64, C)
    for t in range(ce // 384):
        gacc[384 * t:384 * t + 384] = lax.dot_general(
            act2[:, :, 384 * t:384 * t + 384].reshape(H * 64, 384), cot_flat, TN_DIMS, preferred_element_type=F32)
    send_rows(0, gacc[...])

    gathered(zn, mz, at_z, lambda p: vbuf, zv, vz_s, vz_r)
    vbuf2 = jnp.sum(zv[...], axis=0)
    xv[mx] = vbuf2
    spread(xn, mx, at_x, lambda p: xv.at[mx], xv, vx_s, vx_r)
    gathered(xn, mx, at_x, lambda p: xv.at[mx], xv, vx_s, vx_r)
    cv[ch] = jnp.sum(xv[...], axis=0)
    spread(ch_n, ch, at_ch, lambda p: cv.at[ch], cv, vc_s, vc_r)
    gathered(ch_n, ch, at_ch, lambda p: cv.at[ch], cv, vc_s, vc_r)
    gathered(ch_n, ch, at_ch, lambda p: se_ref, sebuf, se_s, se_r)

    area = float(rows_n * H * yn * 2 * W)
    pooled, gate_grad, weights = [], [], []
    for core in (0, 1):
        total = cv[core]
        for q in range(1, yn):
            total = total + cv[2 * q + core]
        pooled.append(jnp.concatenate([total[t:t + 1] for t in range(nt)], axis=1) * (1.0 / area))
        gate_grad.append(jnp.concatenate([total[8 + t:9 + t] for t in range(nt)], axis=1))
        weights.append(jnp.concatenate([sebuf[2 * q + core] for q in range(yn)], axis=0))
    half = lax.broadcasted_iota(jnp.int32, (1, 128), 1) < 64

    def down(vectors):
        total = jnp.zeros((1, 128), F32)
        for core in (0, 1):
            total = total + jnp.sum(jnp.dot(split3(vectors[core]), weights[core], preferred_element_type=F32), axis=0, keepdims=True)
        return total

    def up(vector, core):
        return jnp.sum(lax.dot_general(split3(vector), weights[core], NT_DIMS, preferred_element_type=F32), axis=0, keepdims=True)

    squeeze_pre = jnp.where(half, down(pooled), 0.0)
    squeeze_sig = sigm(squeeze_pre)
    squeeze_act = squeeze_pre * squeeze_sig
    shifted = pltpu.roll(jnp.broadcast_to(squeeze_act, (8, 128)), 64, 1)[0:1]
    gates = [sigm(up(shifted, core)) for core in (0, 1)]
    excite = [gate_grad[core] * gates[core] * (1.0 - gates[core]) for core in (0, 1)]
    back = pltpu.roll(jnp.broadcast_to(down(excite), (8, 128)), 64, 1)[0:1]
    squeeze_slope = squeeze_sig * (1.0 + squeeze_pre * (1.0 - squeeze_sig))
    grad_squeeze = jnp.where(half, back * squeeze_slope, 0.0)

    def own(values):
        return jnp.where(mc == 0, values[0], values[1])

    gate = own(gates)
    grad_pool = own([up(grad_squeeze, core) for core in (0, 1)]) * (1.0 / area)
    for t in range(nt):
        gs[0, t:t + 1] = gate[:, 128 * t:128 * t + 128]
        gs[1, t:t + 1] = grad_pool[:, 128 * t:128 * t + 128]
    vec_ref[0:1] = gate
    vec_ref[1:2] = own(pooled)
    vec_ref[2:3] = own(excite)
    small = jnp.concatenate([squeeze_act, grad_squeeze] + [jnp.zeros((1, 128), F32)] * (nt - 2), axis=1)
    vec_ref[3:4] = small
    vec_ref[4:8] = jnp.zeros((4, ce), F32)

    send_z(0)

    @pl.loop(0, H)
    def _(i):
        act2[i] = (act2[i].astype(F32) * gate).astype(BF16)

    def project(source, k, w_all, base, into):
        def part(where):
            rows = source[:, where].reshape(H * W, ce)
            return jnp.dot(rows, w_all, preferred_element_type=F32).reshape(H, W, C)

        posend[k] = part(other).astype(BF16)
        copy(posend.at[k], porecv.at[k], po_s.at[k], po_r.at[k], sib).start()
        into[...] = part(mine)

    def projected(k, base, total, into):
        copy(posend.at[k], porecv.at[k], po_s.at[k], po_r.at[k], sib).wait()
        into[...] = (base[...].astype(F32) + (total[...] + porecv[k].astype(F32))).astype(BF16)

    project(act2, 0, wbuf[:, 1].reshape(ce, C), x_ref, xf.at[0:H, 0:W])
    send_x(0)

    place = lax.broadcasted_iota(jnp.int32, (PW, 128), 0)
    off_left = jnp.where(left_ok, PW, PW - 1)
    off_right = jnp.where(right_ok, 0, 1)
    inside = jnp.where((place < 64) | ((place == 64) & (off_right == 0)) | ((place == PW - 1) & (off_left == PW)), 1.0, 0.0)

    @pl.loop(0, nt)
    def _(t):
        lanes = pl.ds(pl.multiple_of(t * 128, 128), 128)
        taps = [ktile[t, k:k + 1] for k in range(9)]
        gate_t = gs[0, pl.ds(t, 1)]
        pool_t = gs[1, pl.ds(t, 1)]

        @pl.loop(0, H + 2)
        def _(i):
            keep = jnp.where(((i > 0) | top_ok) & ((i < H + 1) | low_ok), 1.0, 0.0)
            gh[t, i] = (gh[t, i] * gate_t + pool_t) * s2[t, i] * (inside * keep)

        def center(i, sums):
            rows = [gh[t, i + r] for r in range(3)]
            parts = [taps[c] * rows[2] + taps[3 + c] * rows[1] + taps[6 + c] * rows[0] for c in range(3)]
            grad = parts[1] + pltpu.roll(parts[0], PW - 1, 0) + pltpu.roll(parts[2], 1, 0)
            full = grad[0:64] * s1[t, i + 2, 0:64]
            ge[i, :, lanes] = full.astype(BF16)
            here = jnp.concatenate([rows[1][0:64], jnp.zeros((8, 128), F32)], axis=0)
            moved = [pltpu.roll(here, PW - 1, 0), here, pltpu.roll(here, 1, 0)]
            fresh = []
            for r in range(3):
                act = a1[t, i + 1 + r]
                for c in range(3):
                    fresh.append(sums[3 * r + c] + jnp.sum((moved[c] * act).reshape(9, 8, 128), axis=0))
            return tuple(fresh)

        sums = lax.fori_loop(0, H, center, (jnp.zeros((8, 128), F32),) * 9)
        dkacc[t] = jnp.concatenate(
            [jnp.sum(part, axis=0, keepdims=True) for part in sums] + [jnp.zeros((7, 128), F32)], axis=0)

    send_back(0)
    x_flat = xnat[...].reshape(H * 64, C)
    for t in range(ce // 384):
        gacc[384 * t:384 * t + 384] = lax.dot_general(
            ge[:, :, 384 * t:384 * t + 384].reshape(H * 64, 384), x_flat, TN_DIMS, preferred_element_type=F32)
    send_rows(1, gacc[...])
    dksend[...] = jnp.concatenate([dkacc[t] for t in range(nt)], axis=1).astype(BF16)
    spread(yn, my, at_y, lambda p: dksend, dkyr, ky_s, ky_r)
    dkyr[my] = dksend[...]
    project(ge, 1, wbuf[:, 0].reshape(ce, C), c_ref, cf.at[0:H, 0:W])

    send_z(1)
    gathered(yn, my, at_y, lambda p: dksend, dkyr, ky_s, ky_r)
    total = dkyr[0].astype(F32)
    for q in range(1, yn):
        total = total + dkyr[q].astype(F32)
    mine_k = total[:, 0:S]
    for q in range(1, yn):
        mine_k = jnp.where(my == q, total[:, S * q:S * q + S], mine_k)
    dkzs[...] = jnp.concatenate([mine_k, jnp.zeros((16, 256 - S), F32)], axis=1).astype(BF16)
    spread(zn, mz, at_z, lambda p: dkzs, dkzr, kz_s, kz_r)
    dkzr[mz] = dkzs[...]
    projected(0, x_ref, xf.at[0:H, 0:W], out_ref)
    whole(0, dwp_ref)
    send_x(1)
    gathered(zn, mz, at_z, lambda p: dkzs, dkzr, kz_s, kz_r)
    total = dkzr[0].astype(F32)
    for q in range(1, zn):
        total = total + dkzr[q].astype(F32)
    dkxs[...] = total.astype(BF16)
    spread(xn, mx, at_x, lambda p: dkxs, dkxr, kx_s, kx_r)
    dkxr[mx] = dkxs[...]
    projected(1, c_ref, cf.at[0:H, 0:W], din_ref)
    send_back(1)
    gathered(xn, mx, at_x, lambda p: dkxs, dkxr, kx_s, kx_r)
    total = dkxr[0].astype(F32)
    for q in range(1, xn):
        total = total + dkxr[q].astype(F32)
    dk_ref[...] = total
    whole(1, dwe_ref)


def per_device(inputs, w_expand, kernel, w_se1, w_se2, w_project, cotangent):
    rows_n, ch_n = lax.axis_size("rows"), lax.axis_size("ch")
    zn = CHIPS_Z if rows_n % CHIPS_Z == 0 else 2
    xn, yn = rows_n // zn, ch_n // 2
    ce = S * yn
    nt = ce // 128
    zr = S // (zn // 2)
    grad_scale = 1.0 / math.sqrt(rows_n * H * ch_n * W)
    weights = jnp.stack([w_expand.T, w_project])
    se = jnp.concatenate([w_se1, w_se2.T], axis=1)
    taps = jnp.pad(kernel, ((0, 7), (0, 256 - S)))
    vmem, dma = pltpu.VMEM, pltpu.SemaphoreType.DMA
    scratch = [
        vmem((H, W, C), BF16), vmem((H, W, C), BF16),
        vmem((2, 3 * W, C), BF16), vmem((2, 2, 3 * W, C), BF16),
        vmem((3 * H, C), BF16), vmem((2, 3, 3 * H, C), BF16),
        vmem((yn, 2, S, C), BF16), vmem((ch_n, S, 128), BF16), vmem((yn, 16, 256), BF16),
        vmem((H + 4, PW, C), F32), vmem((H + 2, PW, C), F32),
        vmem(((H + 4) * PW, C), BF16), vmem(((H + 2) * PW, C), BF16),
        vmem((H, 64, C), BF16), vmem((H, 64, C), BF16),
        vmem((nt, H + 4, PW, 128), F32), vmem((nt, H + 4, PW, 128), F32),
        vmem((nt, H + 2, PW, 128), F32), vmem((nt, H + 2, PW, 128), F32),
        vmem((H, 64, ce), BF16), vmem((H, 64, ce), BF16),
        vmem((nt, 16, 128), F32), vmem((ce, C), F32), vmem((nt, 16, 128), F32),
        vmem((16, 128), F32), vmem((zn, 16, 128), F32), vmem((xn, 16, 128), F32), vmem((ch_n, 16, 128), F32),
        vmem((2, 8, 128), F32),
        vmem((2, yn, S, C), BF16), vmem((2, yn, S, C), BF16),
        vmem((2, zn, zr, 128), BF16), vmem((2, zn, zr, 128), BF16),
        vmem((2, xn, zr, 128), BF16), vmem((2, 2, zr, 128), BF16), vmem((2, zn, zr, 128), BF16),
        vmem((16, ce), BF16), vmem((yn, 16, ce), BF16),
        vmem((zn, 16, 256), BF16), vmem((16, 256), BF16), vmem((xn, 16, 256), BF16), vmem((16, 256), BF16),
        vmem((2, H, W, C), BF16), vmem((2, H, W, C), BF16),
        dma((2,)), dma((2,)), dma((2, 2)), dma((2, 2)), dma((3, 2)), dma((2, 3)),
        dma((yn,)), dma((yn,)), dma((ch_n,)), dma((ch_n,)), dma((yn,)), dma((yn,)),
        dma((zn,)), dma((zn,)), dma((xn,)), dma((xn,)), dma((ch_n,)), dma((ch_n,)),
        dma((2, yn)), dma((2, yn)), dma((2, zn)), dma((2, zn)), dma((2, xn)), dma((2, xn)), dma((2, zn)), dma((2, zn)),
        dma((yn,)), dma((yn,)), dma((zn,)), dma((zn,)), dma((xn,)), dma((xn,)),
        dma((2,)), dma((2,)),
    ]
    in_vmem = pl.BlockSpec(memory_space=pltpu.VMEM)
    output, d_input, d_expand_t, d_project, d_taps, vec = pl.pallas_call(
        functools.partial(fused, rows_n, ch_n),
        out_shape=(
            jax.ShapeDtypeStruct((H, W, C), BF16), jax.ShapeDtypeStruct((H, W, C), BF16),
            jax.ShapeDtypeStruct((S, C), F32), jax.ShapeDtypeStruct((S, C), F32),
            jax.ShapeDtypeStruct((16, 256), F32), jax.ShapeDtypeStruct((8, ce), F32)),
        in_specs=[in_vmem] * 5,
        out_specs=(in_vmem,) * 6,
        scratch_shapes=scratch,
        compiler_params=pltpu.CompilerParams(
            collective_id=0, has_side_effects=True, vmem_limit_bytes=56 * 1024 * 1024),
    )(inputs[0], cotangent[0], weights, se, taps)
    start = (lax.axis_index("ch") // 2) * S
    own = lax.dynamic_slice_in_dim(vec, start, S, axis=1)
    gate, pooled, excite = own[0], own[1], own[2]
    squeeze_act, grad_squeeze = vec[3, 0:64], vec[3, 128:192]
    return (
        output[None], d_input[None], d_expand_t.T * grad_scale, d_taps[0:9, 0:S] * grad_scale,
        jnp.outer(pooled, grad_squeeze) * grad_scale, jnp.outer(squeeze_act, excite) * grad_scale,
        d_project * (gate[:, None] * grad_scale))


def solution(mesh):
    return jax.shard_map(
        per_device,
        mesh=mesh,
        in_specs=(
            P(None, "rows", "ch", None),
            P(None, "ch"),
            P(None, "ch"),
            P("ch", None),
            P(None, "ch"),
            P("ch", None),
            P(None, "rows", "ch", None),
        ),
        out_specs=(
            P(None, "rows", "ch", None),
            P(None, "rows", "ch", None),
            P(None, "ch"),
            P(None, "ch"),
            P("ch", None),
            P(None, "ch"),
            P("ch", None),
        ),
        check_vma=False,
    )
```

time: 424 us -> 102 us (0.24)
  blocking collectives: 236 us -> 0 us
  waiting for transfers between devices: 113 us -> 0 us
  Pallas kernels: 0 us -> 90 us
  matrix products: 22.7 us -> 0 us
  other arithmetic: 26.6 us -> 6.17 us
  between operations: 14 us -> 0.69 us
  starting transfers between devices: 7.54 us -> 0 us
  local copies, waits for them, and re-layouts: 0.15 us -> 4.7 us
    psum x4 -> x0, blocking collectives: 236 us -> none  [the longest x1 138 us: per_device(): lax.psum(scaled[1].astype(jnp.bfloat16), 'rows').astype(jnp.float32)]
    pallas_call x0 -> x1, Pallas kernels: none -> 90 us  [per_device(): pl.pallas_call(functools.partial(fused, rows_n, ch_n), out_shape=(jax.Sha...]
    reduce_scatter x2 -> x0, waiting for transfers between devices: 57.7 us -> none  [the longest x1 35.9 us: column_step(): lax.psum_scatter(back_part.astype(jnp.bfloat16), 'ch', scatter_dimension=...]
    all_gather x2 -> x0, waiting for transfers between devices: 44.5 us -> none  [the longest x1 30.8 us: column_step(): whole_in = lax.all_gather(image, 'ch', axis=1, tiled=True)]
    dot_general x10 -> x0, matrix products: 22.7 us -> none  [the longest x1 9.68 us: column_step(): jnp.dot(flat_grad, w_project.T, preferred_element_type=jnp.float32)]
    convert_element_type x9 -> x0, other arithmetic: 10.5 us -> none  [the longest x1 5.32 us: column_step(): (grad_act_one * silu_slope(expand_pre)).astype(jnp.bfloat16)]
    ppermute x4 -> x0, waiting for transfers between devices: 9.16 us -> none  [the longest x2 8.03 us: extended(): lax.ppermute(lax.slice_in_dim(block, 0, width, axis=dim), axis, backward)]
    reduce_sum x1 -> x0, other arithmetic: 8.91 us -> none  [tap_sums(): parts.append(jnp.sum(grad_vals * window, axis=(0, 1)))]
  transfers between devices with their start and end apart: 9 -> 0, of which waited for: 7 -> 0; matrix products, arithmetic and copies ran while one was open for 5% -> 0% of each run, Pallas kernels for 0% -> 0%
where the time goes in v1:
time: 102 us
  Pallas kernels  90 us (88%)
  other arithmetic  6.17 us (6%)
  local copies, waits for them, and re-layouts  4.7 us (5%)
    pallas_call x1, Pallas kernels, per_device(): pl.pallas_call(functools.partial(fused, rows_n, ch_n), out_shape=(jax.Sha...  90 us
    unnamed x20, local copies, waits for them, and re-layouts  3.41 us

profile of v1, /device:TPU:8, one launch (start us, length us, event | category | flops | bytes accessed | tf_op | source)
XLA Modules:
  0.0 101.6 jit_solution(17758318733195308827)
XLA Ops:
  0.6 0.0 copy-start.4
  0.7 0.0 copy-start.7
  0.7 0.7 copy-done.7
  1.4 0.6 pad.4.tap_ref
  2.0 0.0 copy-done.4
  2.0 0.0 copy-start.5
  2.0 0.1 copy.15
  2.1 0.6 copy-done.5
  2.7 0.0 copy-start.2
  2.7 0.0 copy-start.3
  2.7 0.1 copy.14
  2.8 0.7 pad_maximum_fusion.1.se_ref
  3.6 0.1 copy-done.2
  3.6 0.0 copy-done.3
  3.7 0.7 pad_maximum_fusion.w_ref
  4.4 90.0 %shard_map.126 = (bf16[16,32,256]{2,1,0:T(8,128)(2,1)}, bf16[16,32,256]{2,1,0:T(8,128)(2,1)}, f32[192,256]{1,0:T(8,128)}, f32[192,256]{1,0:T(8,128)}, f32[16,256]{1,0:T(8,128)}, /*index=5*/f32[8,768]{1,0:T(8,128)}) custom-call(bf16[16,32,256]{2,1,0:T(8,128)(2,1)} %bitcast.18, bf16[16,32,256]{2,1,0:T(8,128)(2,1)} %bitcast.19, ...), custom_call_target="tpu_custom_call" | custom-call | tf_op jit(solution)/shard_map/pallas_call | solution.py:502
  94.4 0.7 slice_bitcast_fusion
  95.0 0.9 dynamic-slice_multiply_fusion
  95.9 0.0 copy-start.6
  95.9 0.0 copy-start.1
  95.9 1.8 %multiply_bitcast_fusion = (f32[256,192]{0,1:T(8,128)}, f32[192,256]{1,0:T(8,128)}) fusion(f32[192,256]{1,0:T(8,128)} %get-tuple-element.15, f32[192,256]{1,0:T(8,128)} %get-tuple-element.18, f32[192]{0:T(256)S(1)} %bitcast.27), kind=kLoop, calls=%fused_computation.1 | loop fusion | flops 98304 | bytes 787200 | tf_op jit(solution)/shard_map/mul | solution.py:519
  97.8 0.0 copy-done.6
  97.8 0.6 slice_multiply_fusion
  98.4 0.7 multiply_multiply_fusion
  99.1 0.7 multiply_multiply_fusion.1
  99.8 0.0 copy-done.1
  99.8 0.0 copy-start
  99.8 0.7 copy.18
  100.5 0.3 copy-done
  100.9 0.7 copy.19
Async XLA Ops:
  0.6 1.3 %copy-start.4 = (bf16[192,64]{0,1:T(8,128)(2,1)S(1)}, bf16[192,64]{0,1:T(8,128)(2,1)}, u32[]{:S(2)}) copy-start(bf16[192,64]{0,1:T(8,128)(2,1)} %param.10) | copy-start | bytes 73732
  0.7 0.7 copy-start.7
  2.0 0.8 copy-start.5
  2.7 0.9 copy-start.2
  2.7 0.9 copy-start.3
  95.9 1.8 %copy-start.6 = (f32[16,256]{1,0:T(8,128)S(1)}, f32[16,256]{1,0:T(8,128)}, u32[]{:S(2)}) copy-start(f32[16,256]{1,0:T(8,128)} %get-tuple-element.16) | copy-start | bytes 49156
  95.9 3.9 %copy-start.1 = (bf16[16,32,256]{2,1,0:T(8,128)(2,1)S(1)}, bf16[16,32,256]{2,1,0:T(8,128)(2,1)}, u32[]{:S(2)}) copy-start(bf16[16,32,256]{2,1,0:T(8,128)(2,1)} %get-tuple-element.13) | copy-start | bytes 786436
  99.8 1.0 %copy-start = (bf16[16,32,256]{2,1,0:T(8,128)(2,1)S(1)}, bf16[16,32,256]{2,1,0:T(8,128)(2,1)}, u32[]{:S(2)}) copy-start(bf16[16,32,256]{2,1,0:T(8,128)(2,1)} %get-tuple-element.14) | copy-start | bytes 786436

commit v2 on v1

--- a/solution.py
+++ b/solution.py
@@ -34,15 +34,28 @@
     return 0.5 * jnp.tanh(0.5 * v) + 0.5
 
 
-def fused(rows_n, ch_n, x_ref, c_ref, w_ref, se_ref, tap_ref,
-          out_ref, din_ref, dwe_ref, dwp_ref, dk_ref, vec_ref,
-          xsib, csib, rowsend, rowbuf, colsend, colbuf, wbuf, sebuf, tapbuf,
+def pairs3(left, right):
+    def three(row):
+        hi = row.astype(BF16).astype(F32)
+        mid = (row - hi).astype(BF16).astype(F32)
+        return hi, mid, row - hi - mid
+
+    a, b = three(left), three(right)
+    lefts = jnp.concatenate([a[k] for k in (0, 0, 1, 1, 0, 2, 1, 2)], axis=0).astype(BF16)
+    rights = jnp.concatenate([b[k] for k in (0, 1, 0, 1, 2, 0, 2, 1)], axis=0).astype(BF16)
+    return lefts, rights
+
+
+def fused(rows_n, ch_n, scale, x_in, we_ref, tap_ref, se1_ref, se2_ref, wp_ref, c_in,
+          out_ref, din_ref, dwe_ref, dk_ref, dse1_ref, dse2_ref, dwp_ref,
+          xsib, csib, rowsend, rowbuf, colsend, colbuf, wesend, webuf, wpbuf, sesend, sebuf, tapsend, tapbuf,
           xf, cf, xs, cs, xnat, cnat, a1, s1, gh, s2, act2, ge, ktile, gacc, dkacc,
           vbuf, zv, xv, cv, gs, ysend, yrecv, zsend, zrecv, xrecv, fsend, frecv,
           dksend, dkyr, dkzr, dkxs, dkxr, dkzs, posend, porecv,
-          sib_s, sib_r, row_s, row_r, col_s, col_r, w_s, w_r, se_s, se_r, tap_s, tap_r,
+          sib_s, sib_r, row_s, row_r, col_s, col_r, we_s, we_r, wp_s, wp_r, se_s, se_r, rel_s, rel_r, tap_s, tap_r,
           vz_s, vz_r, vx_s, vx_r, vc_s, vc_r, gy_s, gy_r, gz_s, gz_r, gx_s, gx_r, gf_s, gf_r,
           ky_s, ky_r, kz_s, kz_r, kx_s, kx_r, po_s, po_r):
+    x_ref, c_ref = x_in.at[0], c_in.at[0]
     zn = CHIPS_Z if rows_n % CHIPS_Z == 0 else 2
     xn = rows_n // zn
     yn = ch_n // 2
@@ -88,6 +101,18 @@
             peer = lax.rem(me + step, n)
             copy(src(peer), land.at[peer], ssem.at[step - 1], rsem.at[peer], at(peer)).wait()
 
+    pair_mine = my // 2
+    near = my + 1 - 2 * lax.rem(my, 2)
+    far = [lax.rem(pair_mine + b, pairs) * 2 + k for b in range(1, pairs) for k in (0, 1)]
+
+    def to_y(peers, first, src, land, ssem, rsem):
+        for k, peer in enumerate(peers):
+            copy(src(peer), land.at[my], ssem.at[first + k], rsem.at[my], at_y(peer)).start()
+
+    def from_y(peers, first, src, land, ssem, rsem):
+        for k, peer in enumerate(peers):
+            copy(src(peer), land.at[peer], ssem.at[first + k], rsem.at[peer], at_y(peer)).wait()
+
     barrier = pltpu.get_barrier_semaphore()
     partners = [at_ch(lax.rem(ch + s, ch_n)) for s in range(1, ch_n)]
     partners += [at_z(lax.rem(mz + s, zn)) for s in range(1, zn)]
@@ -109,6 +134,13 @@
     ci = lax.broadcasted_iota(jnp.int32, (H, H * W), 1)
     pick = (ci == ri * W + mc * (W - 1)).astype(F32).astype(BF16)
     colsend[2 * H:3 * H] = jnp.dot(pick, c_ref[...].reshape(H * W, C), preferred_element_type=F32).astype(BF16)
+
+    eye = (lax.broadcasted_iota(jnp.int32, (S, S), 0) == lax.broadcasted_iota(jnp.int32, (S, S), 1)).astype(F32).astype(BF16)
+    wesend[...] = lax.dot_general(eye, we_ref[...], NT_DIMS, preferred_element_type=F32).astype(BF16)
+    se2_t = lax.dot_general(eye, se2_ref[...], NT_DIMS, preferred_element_type=F32)
+    sesend[...] = jnp.concatenate([se1_ref[...].astype(F32), se2_t], axis=1).astype(BF16)
+    tap_rows = jnp.concatenate([tap_ref[...].astype(F32), jnp.zeros((7, S), F32)], axis=0)
+    tapsend[...] = jnp.concatenate([tap_rows, jnp.zeros((16, 256 - S), F32)], axis=1).astype(BF16)
 
     pl.semaphore_wait(barrier, len(partners))
 
@@ -128,29 +160,31 @@
             where = (dev_row(dr), dev_y(2 * mc - 1) * 2 + core)
             col_copies.append((copy(colsend, colbuf.at[side, 2 - i], col_s.at[i, core], col_r.at[side, 2 - i], where),
                                copy(colsend, colbuf.at[core, i], col_s.at[i, core], col_r.at[core, i], where)))
-    for sent in sib_copies:
-        sent.start()
+    sib_copies[0].start()
     for sent, _ in row_copies + col_copies:
         sent.start()
-    spread(yn, my, at_y, lambda p: tap_ref, tapbuf, tap_s, tap_r)
-    spread(yn, my, at_y, lambda p: w_ref, wbuf, w_s, w_r)
-    spread(ch_n, ch, at_ch, lambda p: se_ref, sebuf, se_s, se_r)
-
-    wbuf[my] = w_ref[...]
-    tapbuf[my] = tap_ref[...]
-    sebuf[ch] = se_ref[...]
+    to_y([near], 0, lambda p: wesend, webuf, we_s, we_r)
+    spread(yn, my, at_y, lambda p: tapsend, tapbuf, tap_s, tap_r)
+    sib_copies[1].start()
+    to_y(far, 1, lambda p: wesend, webuf, we_s, we_r)
+    to_y([near] + far, 0, lambda p: wp_ref, wpbuf, wp_s, wp_r)
+    spread(yn, my, at_y, lambda p: sesend, sebuf.at[mc], se_s, se_r)
+    relay = copy(sebuf.at[mc], sebuf.at[mc], rel_s.at[0], rel_r.at[mc], sib)
+    relayed = copy(sebuf.at[mc], sebuf.at[oc], rel_s.at[0], rel_r.at[oc], sib)
+
+    webuf[my] = wesend[...]
+    wpbuf[my] = wp_ref[...]
+    tapbuf[my] = tapsend[...]
+    sebuf[mc, my] = sesend[...]
     mine = pl.ds(pl.multiple_of(mc * W, W), W)
     other = pl.ds(pl.multiple_of(oc * W, W), W)
     xf[2:2 + H, mine] = x_ref[...].astype(F32)
     cf[1:1 + H, mine] = c_ref[...].astype(F32)
     xnat[:, mine] = x_ref[...]
     cnat[:, mine] = c_ref[...]
-    for sent in sib_copies:
-        sent.wait()
+    sib_copies[0].wait()
     xf[2:2 + H, other] = xsib[...].astype(F32)
-    cf[1:1 + H, other] = csib[...].astype(F32)
     xnat[:, other] = xsib[...]
-    cnat[:, other] = csib[...]
     for _, landed in row_copies + col_copies:
         landed.wait()
 
@@ -182,28 +216,23 @@
         return jnp.dot(hit, cols, preferred_element_type=F32).reshape(height, 8, C)
 
     xf[:, 64:72] = rim(H + 4, 2, lambda k: jnp.where(k >= 6, k - 6, -1), lambda k: jnp.where(k < 2, k, -1))
-    cf[:, 64:72] = rim(H + 2, 1, lambda k: jnp.where(k == 7, 2, -1), lambda k: jnp.where(k == 0, 2, -1))
 
     @pl.loop(0, (H + 4) // 2)
     def _(i):
         at = pl.ds(pl.multiple_of(i * 2 * PW, 2 * PW), 2 * PW)
         xs[at] = xf[pl.ds(i * 2, 2)].reshape(2 * PW, C).astype(BF16)
 
-    @pl.loop(0, (H + 2) // 2)
-    def _(i):
-        at = pl.ds(pl.multiple_of(i * 2 * PW, 2 * PW), 2 * PW)
-        cs[at] = cf[pl.ds(i * 2, 2)].reshape(2 * PW, C).astype(BF16)
-
-    gathered(yn, my, at_y, lambda p: tap_ref, tapbuf, tap_s, tap_r)
+    gathered(yn, my, at_y, lambda p: tapsend, tapbuf, tap_s, tap_r)
     wide = jnp.concatenate([tapbuf[q].astype(F32)[:, 0:S] for q in range(yn)], axis=1)
     for t in range(nt):
         ktile[t] = wide[:, 128 * t:128 * t + 128]
-    gathered(yn, my, at_y, lambda p: w_ref, wbuf, w_s, w_r)
+    from_y([near], 0, lambda p: wesend, webuf, we_s, we_r)
 
     for b in range(pairs):
-        pair = lax.rem(my // 2 + b, pairs)
-        w_exp = wbuf[pl.ds(pair * 2, 2), 0].reshape(2 * S, C)
-        w_pro = wbuf[pl.ds(pair * 2, 2), 1].reshape(2 * S, C)
+        pair = lax.rem(pair_mine + b, pairs)
+        if b == 1:
+            from_y(far, 1, lambda p: wesend, webuf, we_s, we_r)
+        w_exp = webuf[pl.ds(pair * 2, 2)].reshape(2 * S, C)
 
         @pl.loop(0, (H + 4) // 2)
         def _(i):
@@ -216,13 +245,6 @@
                 a1[pair * 3 + t, pl.ds(i * 2, 2)] = act[:, 128 * t:128 * t + 128].reshape(2, PW, 128)
                 s1[pair * 3 + t, pl.ds(i * 2, 2)] = slope[:, 128 * t:128 * t + 128].reshape(2, PW, 128)
 
-        @pl.loop(0, (H + 2) // 2)
-        def _(i):
-            at = pl.ds(pl.multiple_of(i * 2 * PW, 2 * PW), 2 * PW)
-            back = lax.dot_general(cs[at], w_pro, NT_DIMS, preferred_element_type=F32)
-            for t in range(3):
-                gh[pair * 3 + t, pl.ds(i * 2, 2)] = back[:, 128 * t:128 * t + 128].reshape(2, PW, 128)
-
         @pl.loop(0, 3)
         def _(t3):
             t = pair * 3 + t3
@@ -238,20 +260,34 @@
                 s2[t, i] = sig * (1.0 + (pre - act))
                 return act[0:64]
 
-            def center(i, sums):
-                pool, gate_sum = sums
+            def center(i, pool):
                 act = one_row(i)
                 act2[i - 1, :, lanes] = act.astype(BF16)
-                pool = pool + jnp.sum(act.reshape(8, 8, 128), axis=0)
-                gate_sum = gate_sum + jnp.sum((act * gh[t, i, 0:64]).reshape(8, 8, 128), axis=0)
-                return pool, gate_sum
+                return pool + jnp.sum(act.reshape(8, 8, 128), axis=0)
 
             one_row(0)
             one_row(H + 1)
-            zero = jnp.zeros((8, 128), F32)
-            pool, gate_sum = lax.fori_loop(1, H + 1, center, (zero, zero))
+            pool = lax.fori_loop(1, H + 1, center, jnp.zeros((8, 128), F32))
             vbuf[pl.ds(t, 1)] = jnp.sum(pool, axis=0, keepdims=True)
-            vbuf[pl.ds(8 + t, 1)] = jnp.sum(gate_sum, axis=0, keepdims=True)
+
+    sib_copies[1].wait()
+    cf[1:1 + H, other] = csib[...].astype(F32)
+    cnat[:, other] = csib[...]
+    cot_flat = cnat[...].reshape(H * 64, C)
+    from_y([near] + far, 0, lambda p: wp_ref, wpbuf, wp_s, wp_r)
+    ones = jnp.ones((8, C), F32).astype(BF16)
+    for t in range(ce // 384):
+        rows = lax.dot_general(
+            act2[:, :, 384 * t:384 * t + 384].reshape(H * 64, 384), cot_flat, TN_DIMS, preferred_element_type=F32)
+        gacc[384 * t:384 * t + 384] = rows
+        prod = rows * wpbuf[2 * t:2 * t + 2].reshape(384, C).astype(F32)
+        hi = prod.astype(BF16)
+        rest = prod - hi.astype(F32)
+        mid = rest.astype(BF16)
+        low = (rest - mid.astype(F32)).astype(BF16)
+        gate_sum = sum(lax.dot_general(ones, part, NT_DIMS, preferred_element_type=F32) for part in (hi, mid, low))
+        for k in range(3):
+            vbuf[8 + 3 * t + k:9 + 3 * t + k] = gate_sum[0:1, 128 * k:128 * k + 128]
 
     for t in range(nt, 8):
         vbuf[t:t + 1] = jnp.zeros((1, 128), F32)
@@ -262,11 +298,11 @@
 
     def send_rows(g, value):
         ysend[g] = value.reshape(yn, S, C).astype(BF16)
-        spread(yn, my, at_y, lambda p: ysend.at[g, p], yrecv.at[g], gy_s.at[g], gy_r.at[g])
+        to_y([near] + far, 0, lambda p: ysend.at[g, p], yrecv.at[g], gy_s.at[g], gy_r.at[g])
         yrecv[g, my] = ysend[g, my]
 
     def send_z(g):
-        gathered(yn, my, at_y, lambda p: ysend.at[g, p], yrecv.at[g], gy_s.at[g], gy_r.at[g])
+        from_y([near] + far, 0, lambda p: ysend.at[g, p], yrecv.at[g], gy_s.at[g], gy_r.at[g])
         total = yrecv[g, 0].astype(F32)
         for q in range(1, yn):
             total = total + yrecv[g, q].astype(F32)
@@ -298,21 +334,38 @@
         for q in range(zn):
             into[zr * (q // 2):zr * (q // 2) + zr, 128 * (q % 2):128 * (q % 2) + 128] = frecv[g, q].astype(F32)
 
-    cot_flat = cnat[...].reshape(H * 64, C)
-    for t in range(ce // 384):
-        gacc[384 * t:384 * t + 384] = lax.dot_general(
-            act2[:, :, 384 * t:384 * t + 384].reshape(H * 64, 384), cot_flat, TN_DIMS, preferred_element_type=F32)
     send_rows(0, gacc[...])
+    gathered(yn, my, at_y, lambda p: sesend, sebuf.at[mc], se_s, se_r)
+    relay.start()
+
+    cf[:, 64:72] = rim(H + 2, 1, lambda k: jnp.where(k == 7, 2, -1), lambda k: jnp.where(k == 0, 2, -1))
+
+    @pl.loop(0, (H + 2) // 2)
+    def _(i):
+        at = pl.ds(pl.multiple_of(i * 2 * PW, 2 * PW), 2 * PW)
+        cs[at] = cf[pl.ds(i * 2, 2)].reshape(2 * PW, C).astype(BF16)
+
+    def hidden_grad(pair):
+        w_pro = wpbuf[2 * pair:2 * pair + 2].reshape(2 * S, C)
+
+        @pl.loop(0, (H + 2) // 2)
+        def _(i):
+            at = pl.ds(pl.multiple_of(i * 2 * PW, 2 * PW), 2 * PW)
+            back = lax.dot_general(cs[at], w_pro, NT_DIMS, preferred_element_type=F32)
+            for t in range(3):
+                gh[pair * 3 + t, pl.ds(i * 2, 2)] = back[:, 128 * t:128 * t + 128].reshape(2, PW, 128)
 
     gathered(zn, mz, at_z, lambda p: vbuf, zv, vz_s, vz_r)
-    vbuf2 = jnp.sum(zv[...], axis=0)
-    xv[mx] = vbuf2
+    xv[mx] = jnp.sum(zv[...], axis=0)
     spread(xn, mx, at_x, lambda p: xv.at[mx], xv, vx_s, vx_r)
+    hidden_grad(0)
     gathered(xn, mx, at_x, lambda p: xv.at[mx], xv, vx_s, vx_r)
     cv[ch] = jnp.sum(xv[...], axis=0)
     spread(ch_n, ch, at_ch, lambda p: cv.at[ch], cv, vc_s, vc_r)
+    for pair in range(1, pairs):
+        hidden_grad(pair)
     gathered(ch_n, ch, at_ch, lambda p: cv.at[ch], cv, vc_s, vc_r)
-    gathered(ch_n, ch, at_ch, lambda p: se_ref, sebuf, se_s, se_r)
+    relayed.wait()
 
     area = float(rows_n * H * yn * 2 * W)
     pooled, gate_grad, weights = [], [], []
@@ -322,7 +375,7 @@
             total = total + cv[2 * q + core]
         pooled.append(jnp.concatenate([total[t:t + 1] for t in range(nt)], axis=1) * (1.0 / area))
         gate_grad.append(jnp.concatenate([total[8 + t:9 + t] for t in range(nt)], axis=1))
-        weights.append(jnp.concatenate([sebuf[2 * q + core] for q in range(yn)], axis=0))
+        weights.append(sebuf[core].reshape(ce, 128))
     half = lax.broadcasted_iota(jnp.int32, (1, 128), 1) < 64
 
     def down(vectors):
@@ -352,20 +405,15 @@
     for t in range(nt):
         gs[0, t:t + 1] = gate[:, 128 * t:128 * t + 128]
         gs[1, t:t + 1] = grad_pool[:, 128 * t:128 * t + 128]
-    vec_ref[0:1] = gate
-    vec_ref[1:2] = own(pooled)
-    vec_ref[2:3] = own(excite)
-    small = jnp.concatenate([squeeze_act, grad_squeeze] + [jnp.zeros((1, 128), F32)] * (nt - 2), axis=1)
-    vec_ref[3:4] = small
-    vec_ref[4:8] = jnp.zeros((4, ce), F32)
-
     send_z(0)
 
-    @pl.loop(0, H)
-    def _(i):
-        act2[i] = (act2[i].astype(F32) * gate).astype(BF16)
-
-    def project(source, k, w_all, base, into):
+    def shard_of(rows):
+        part = rows[:, 0:S]
+        for q in range(1, yn):
+            part = jnp.where(my == q, rows[:, S * q:S * q + S], part)
+        return part
+
+    def project(source, k, w_all, into):
         def part(where):
             rows = source[:, where].reshape(H * W, ce)
             return jnp.dot(rows, w_all, preferred_element_type=F32).reshape(H, W, C)
@@ -376,35 +424,56 @@
 
     def projected(k, base, total, into):
         copy(posend.at[k], porecv.at[k], po_s.at[k], po_r.at[k], sib).wait()
-        into[...] = (base[...].astype(F32) + (total[...] + porecv[k].astype(F32))).astype(BF16)
-
-    project(act2, 0, wbuf[:, 1].reshape(ce, C), x_ref, xf.at[0:H, 0:W])
-    send_x(0)
+        into[0] = (base[...].astype(F32) + (total[...] + porecv[k].astype(F32))).astype(BF16)
 
     place = lax.broadcasted_iota(jnp.int32, (PW, 128), 0)
     off_left = jnp.where(left_ok, PW, PW - 1)
     off_right = jnp.where(right_ok, 0, 1)
     inside = jnp.where((place < 64) | ((place == 64) & (off_right == 0)) | ((place == PW - 1) & (off_left == PW)), 1.0, 0.0)
 
+    x_flat = xnat[...].reshape(H * 64, C)
+    for b in range(pairs):
+        pair = lax.rem(pair_mine + 1 + b, pairs)
+
+        @pl.loop(0, 3)
+        def _(t3):
+            t = pair * 3 + t3
+            lanes = pl.ds(pl.multiple_of(t * 128, 128), 128)
+            taps = [ktile[t, k:k + 1] for k in range(9)]
+            gate_t = gs[0, pl.ds(t, 1)]
+            pool_t = gs[1, pl.ds(t, 1)]
+
+            @pl.loop(0, H + 2)
+            def _(i):
+                keep = jnp.where(((i > 0) | top_ok) & ((i < H + 1) | low_ok), 1.0, 0.0)
+                gh[t, i] = (gh[t, i] * gate_t + pool_t) * s2[t, i] * (inside * keep)
+
+            @pl.loop(0, H)
+            def _(i):
+                rows = [gh[t, i + r] for r in range(3)]
+                parts = [taps[c] * rows[2] + taps[3 + c] * rows[1] + taps[6 + c] * rows[0] for c in range(3)]
+                grad = parts[1] + pltpu.roll(parts[0], PW - 1, 0) + pltpu.roll(parts[2], 1, 0)
+                ge[i, :, lanes] = (grad[0:64] * s1[t, i + 2, 0:64]).astype(BF16)
+
+        lanes3 = pl.ds(pl.multiple_of(pair * 384, 384), 384)
+        rows = lax.dot_general(ge[:, :, lanes3].reshape(H * 64, 384), x_flat, TN_DIMS, preferred_element_type=F32)
+        ysend[1, pl.ds(pair * 2, 2)] = rows.reshape(2, S, C).astype(BF16)
+        if b < pairs - 1:
+            to_y(far, 1, lambda p: ysend.at[1, p], yrecv.at[1], gy_s.at[1], gy_r.at[1])
+            send_x(0)
+        else:
+            to_y([near], 0, lambda p: ysend.at[1, p], yrecv.at[1], gy_s.at[1], gy_r.at[1])
+            yrecv[1, my] = ysend[1, my]
+
+    project(ge, 1, webuf[...].reshape(ce, C), cf.at[0:H, 0:W])
+    if pairs == 1:
+        send_x(0)
+    send_back(0)
+
     @pl.loop(0, nt)
     def _(t):
-        lanes = pl.ds(pl.multiple_of(t * 128, 128), 128)
-        taps = [ktile[t, k:k + 1] for k in range(9)]
-        gate_t = gs[0, pl.ds(t, 1)]
-        pool_t = gs[1, pl.ds(t, 1)]
-
-        @pl.loop(0, H + 2)
-        def _(i):
-            keep = jnp.where(((i > 0) | top_ok) & ((i < H + 1) | low_ok), 1.0, 0.0)
-            gh[t, i] = (gh[t, i] * gate_t + pool_t) * s2[t, i] * (inside * keep)
-
         def center(i, sums):
-            rows = [gh[t, i + r] for r in range(3)]
-            parts = [taps[c] * rows[2] + taps[3 + c] * rows[1] + taps[6 + c] * rows[0] for c in range(3)]
-            grad = parts[1] + pltpu.roll(parts[0], PW - 1, 0) + pltpu.roll(parts[2], 1, 0)
-            full = grad[0:64] * s1[t, i + 2, 0:64]
-            ge[i, :, lanes] = full.astype(BF16)
-            here = jnp.concatenate([rows[1][0:64], jnp.zeros((8, 128), F32)], axis=0)
+            here = jnp.concatenate([gh[t, i + 1, 0:64], jnp.zeros((8, 128), F32)], axis=0)
             moved = [pltpu.roll(here, PW - 1, 0), here, pltpu.roll(here, 1, 0)]
             fresh = []
             for r in range(3):
@@ -417,46 +486,49 @@
         dkacc[t] = jnp.concatenate(
             [jnp.sum(part, axis=0, keepdims=True) for part in sums] + [jnp.zeros((7, 128), F32)], axis=0)
 
-    send_back(0)
-    x_flat = xnat[...].reshape(H * 64, C)
-    for t in range(ce // 384):
-        gacc[384 * t:384 * t + 384] = lax.dot_general(
-            ge[:, :, 384 * t:384 * t + 384].reshape(H * 64, 384), x_flat, TN_DIMS, preferred_element_type=F32)
-    send_rows(1, gacc[...])
     dksend[...] = jnp.concatenate([dkacc[t] for t in range(nt)], axis=1).astype(BF16)
     spread(yn, my, at_y, lambda p: dksend, dkyr, ky_s, ky_r)
     dkyr[my] = dksend[...]
-    project(ge, 1, wbuf[:, 0].reshape(ce, C), c_ref, cf.at[0:H, 0:W])
-
     send_z(1)
+
+    @pl.loop(0, H)
+    def _(i):
+        act2[i] = (act2[i].astype(F32) * gate).astype(BF16)
+
+    project(act2, 0, wpbuf[...].reshape(ce, C), xf.at[0:H, 0:W])
+
+    def summed(parts):
+        total = parts[0].astype(F32)
+        for q in range(1, parts.shape[0]):
+            total = total + parts[q].astype(F32)
+        return total
+
     gathered(yn, my, at_y, lambda p: dksend, dkyr, ky_s, ky_r)
-    total = dkyr[0].astype(F32)
-    for q in range(1, yn):
-        total = total + dkyr[q].astype(F32)
-    mine_k = total[:, 0:S]
-    for q in range(1, yn):
-        mine_k = jnp.where(my == q, total[:, S * q:S * q + S], mine_k)
-    dkzs[...] = jnp.concatenate([mine_k, jnp.zeros((16, 256 - S), F32)], axis=1).astype(BF16)
+    dkzs[...] = jnp.concatenate([shard_of(summed(dkyr)), jnp.zeros((16, 256 - S), F32)], axis=1).astype(BF16)
     spread(zn, mz, at_z, lambda p: dkzs, dkzr, kz_s, kz_r)
     dkzr[mz] = dkzs[...]
-    projected(0, x_ref, xf.at[0:H, 0:W], out_ref)
-    whole(0, dwp_ref)
     send_x(1)
+    projected(1, c_ref, cf.at[0:H, 0:W], din_ref)
     gathered(zn, mz, at_z, lambda p: dkzs, dkzr, kz_s, kz_r)
-    total = dkzr[0].astype(F32)
-    for q in range(1, zn):
-        total = total + dkzr[q].astype(F32)
-    dkxs[...] = total.astype(BF16)
+    dkxs[...] = summed(dkzr).astype(BF16)
     spread(xn, mx, at_x, lambda p: dkxs, dkxr, kx_s, kx_r)
     dkxr[mx] = dkxs[...]
-    projected(1, c_ref, cf.at[0:H, 0:W], din_ref)
     send_back(1)
+
+    own_gate = shard_of(gate)
+    lefts, rights = pairs3(shard_of(own(pooled)), grad_squeeze * scale)
+    dse1_ref[...] = lax.dot_general(lefts, rights, TN_DIMS, preferred_element_type=F32)[:, 0:64]
+    lefts, rights = pairs3(squeeze_act, shard_of(own(excite)) * scale)
+    dse2_ref[...] = lax.dot_general(lefts, rights, TN_DIMS, preferred_element_type=F32)[0:64]
+    gate_wide = lax.dot_general(split3(own_gate * scale), ones, TN_DIMS, preferred_element_type=F32)
+    projected(0, x_ref, xf.at[0:H, 0:W], out_ref)
+    whole(0, gacc.at[0:S])
+    dwp_ref[...] = gacc[0:S] * gate_wide
     gathered(xn, mx, at_x, lambda p: dkxs, dkxr, kx_s, kx_r)
-    total = dkxr[0].astype(F32)
-    for q in range(1, xn):
-        total = total + dkxr[q].astype(F32)
-    dk_ref[...] = total
-    whole(1, dwe_ref)
+    dk_ref[...] = summed(dkxr)[0:9, 0:S] * scale
+    whole(1, gacc.at[S:2 * S])
+    turned = lax.dot_general(gacc[S:2 * S].astype(BF16), eye, TN_DIMS, preferred_element_type=F32)
+    dwe_ref[...] = turned * scale
 
 
 def per_device(inputs, w_expand, kernel, w_se1, w_se2, w_project, cotangent):
@@ -467,15 +539,14 @@
     nt = ce // 128
     zr = S // (zn // 2)
     grad_scale = 1.0 / math.sqrt(rows_n * H * ch_n * W)
-    weights = jnp.stack([w_expand.T, w_project])
-    se = jnp.concatenate([w_se1, w_se2.T], axis=1)
-    taps = jnp.pad(kernel, ((0, 7), (0, 256 - S)))
     vmem, dma = pltpu.VMEM, pltpu.SemaphoreType.DMA
     scratch = [
         vmem((H, W, C), BF16), vmem((H, W, C), BF16),
         vmem((2, 3 * W, C), BF16), vmem((2, 2, 3 * W, C), BF16),
         vmem((3 * H, C), BF16), vmem((2, 3, 3 * H, C), BF16),
-        vmem((yn, 2, S, C), BF16), vmem((ch_n, S, 128), BF16), vmem((yn, 16, 256), BF16),
+        vmem((S, C), BF16), vmem((yn, S, C), BF16), vmem((yn, S, C), BF16),
+        vmem((S, 128), BF16), vmem((2, yn, S, 128), BF16),
+        vmem((16, 256), BF16), vmem((yn, 16, 256), BF16),
         vmem((H + 4, PW, C), F32), vmem((H + 2, PW, C), F32),
         vmem(((H + 4) * PW, C), BF16), vmem(((H + 2) * PW, C), BF16),
         vmem((H, 64, C), BF16), vmem((H, 64, C), BF16),
@@ -492,33 +563,27 @@
         vmem((zn, 16, 256), BF16), vmem((16, 256), BF16), vmem((xn, 16, 256), BF16), vmem((16, 256), BF16),
         vmem((2, H, W, C), BF16), vmem((2, H, W, C), BF16),
         dma((2,)), dma((2,)), dma((2, 2)), dma((2, 2)), dma((3, 2)), dma((2, 3)),
-        dma((yn,)), dma((yn,)), dma((ch_n,)), dma((ch_n,)), dma((yn,)), dma((yn,)),
+        dma((yn,)), dma((yn,)), dma((yn,)), dma((yn,)),
+        dma((yn,)), dma((yn,)), dma((1,)), dma((2,)), dma((yn,)), dma((yn,)),
         dma((zn,)), dma((zn,)), dma((xn,)), dma((xn,)), dma((ch_n,)), dma((ch_n,)),
         dma((2, yn)), dma((2, yn)), dma((2, zn)), dma((2, zn)), dma((2, xn)), dma((2, xn)), dma((2, zn)), dma((2, zn)),
         dma((yn,)), dma((yn,)), dma((zn,)), dma((zn,)), dma((xn,)), dma((xn,)),
         dma((2,)), dma((2,)),
     ]
     in_vmem = pl.BlockSpec(memory_space=pltpu.VMEM)
-    output, d_input, d_expand_t, d_project, d_taps, vec = pl.pallas_call(
-        functools.partial(fused, rows_n, ch_n),
+    return pl.pallas_call(
+        functools.partial(fused, rows_n, ch_n, grad_scale),
         out_shape=(
-            jax.ShapeDtypeStruct((H, W, C), BF16), jax.ShapeDtypeStruct((H, W, C), BF16),
-            jax.ShapeDtypeStruct((S, C), F32), jax.ShapeDtypeStruct((S, C), F32),
-            jax.ShapeDtypeStruct((16, 256), F32), jax.ShapeDtypeStruct((8, ce), F32)),
-        in_specs=[in_vmem] * 5,
-        out_specs=(in_vmem,) * 6,
+            jax.ShapeDtypeStruct((1, H, W, C), BF16), jax.ShapeDtypeStruct((1, H, W, C), BF16),
+            jax.ShapeDtypeStruct((C, S), F32), jax.ShapeDtypeStruct((9, S), F32),
+            jax.ShapeDtypeStruct((S, 64), F32), jax.ShapeDtypeStruct((64, S), F32),
+            jax.ShapeDtypeStruct((S, C), F32)),
+        in_specs=[in_vmem] * 7,
+        out_specs=(in_vmem,) * 7,
         scratch_shapes=scratch,
         compiler_params=pltpu.CompilerParams(
             collective_id=0, has_side_effects=True, vmem_limit_bytes=56 * 1024 * 1024),
-    )(inputs[0], cotangent[0], weights, se, taps)
-    start = (lax.axis_index("ch") // 2) * S
-    own = lax.dynamic_slice_in_dim(vec, start, S, axis=1)
-    gate, pooled, excite = own[0], own[1], own[2]
-    squeeze_act, grad_squeeze = vec[3, 0:64], vec[3, 128:192]
-    return (
-        output[None], d_input[None], d_expand_t.T * grad_scale, d_taps[0:9, 0:S] * grad_scale,
-        jnp.outer(pooled, grad_squeeze) * grad_scale, jnp.outer(squeeze_act, excite) * grad_scale,
-        d_project * (gate[:, None] * grad_scale))
+    )(inputs, w_expand, kernel, w_se1, w_se2, w_project, cotangent)
 
 
 def solution(mesh):

time: 102 us -> 85 us (0.83)
  Pallas kernels: 90 us -> 73.8 us
  other arithmetic: 6.17 us -> 0 us
  local copies, waits for them, and re-layouts: 4.7 us -> 10.2 us
    pallas_call x1, Pallas kernels: 90 us -> 73.8 us  [per_device(): pl.pallas_call(functools.partial(fused, rows_n, ch_n, grad_scale), out_sh...]
    mul x5 -> x0, other arithmetic: 4.75 us -> none  [the longest x1 1.84 us: per_device(): d_expand_t.T * grad_scale]
    unnamed x20 -> x17, local copies, waits for them, and re-layouts: 3.41 us -> 6.81 us
    pallas_call x0 -> x2, local copies, waits for them, and re-layouts: none -> 3.39 us  [per_device(): pl.pallas_call(functools.partial(fused, rows_n, ch_n, grad_scale), out_sh...]
where the time goes in v2:
time: 85 us; the launch traced here: 84.7 us
  Pallas kernels  73.8 us (87%)
  local copies, waits for them, and re-layouts  10.2 us (12%)
    pallas_call x1, Pallas kernels, per_device(): pl.pallas_call(functools.partial(fused, rows_n, ch_n, grad_scale), out_sh...  73.8 us
    unnamed x17, local copies, waits for them, and re-layouts  6.81 us
    pallas_call x2, local copies, waits for them, and re-layouts, per_device(): pl.pallas_call(functools.partial(fused, rows_n, ch_n, grad_scale), out_sh...  3.39 us

profile of v2, /device:TPU:8, one launch (start us, length us, event | category | flops | bytes accessed | tf_op | source)
XLA Modules:
  0.0 84.7 jit_solution(3360204344110064734)
XLA Ops:
  0.6 1.5 %copy.15.se1_ref = bf16[192,64]{1,0:T(8,128)(2,1)} copy(bf16[192,64]{0,1:T(8,128)(2,1)} %param.10) | data formatting | bytes 49152 | tf_op args[3]
  2.1 1.7 %copy.14.we_ref = bf16[256,192]{1,0:T(8,128)(2,1)} copy(bf16[256,192]{0,1:T(8,128)(2,1)} %param.8) | data formatting | bytes 196608 | tf_op args[1]
  3.8 73.8 %shard_map.126 = (bf16[1,16,32,256]{3,2,1,0:T(8,128)(2,1)}, bf16[1,16,32,256]{3,2,1,0:T(8,128)(2,1)}, f32[256,192]{1,0:T(8,128)}, f32[9,192]{1,0:T(8,128)}, f32[...) custom-call(bf16[1,16,32,256]{3,2,1,0:T(8,128)(2,1)} %x_in.1, bf16[256,192]{1,0:T(8,128)(2,1)} %copy.14.we_ref, ...), custom_call_target="tpu_custom_call" | custom-call | tf_op jit(solution)/shard_map/pallas_call | solution.py:574
  77.6 1.6 %copy.17 = f32[192,64]{0,1:T(8,128)} copy(f32[192,64]{1,0:T(8,128)} %get-tuple-element.11) | data formatting | bytes 98304 | tf_op jit(solution)/shard_map/pallas_call | solution.py:574
  79.2 0.0 copy-start.1
  79.2 1.8 %copy.16 = f32[256,192]{0,1:T(8,128)} copy(f32[256,192]{1,0:T(8,128)} %get-tuple-element.9) | data formatting | bytes 393216 | tf_op jit(solution)/shard_map/pallas_call | solution.py:574
  81.0 0.0 copy-done.1
  81.0 0.0 copy-start
  81.0 0.7 copy.23
  81.7 0.3 copy-done
  82.1 0.0 copy-start.4
  82.1 0.0 copy-start.3
  82.1 0.0 copy-start.2
  82.1 0.7 copy.24
  82.8 0.0 copy-done.4
  82.8 0.6 copy.25
  83.4 0.0 copy-done.3
  83.4 0.6 copy.26
  84.0 0.0 copy-done.2
  84.0 0.7 copy.27
Async XLA Ops:
  79.2 1.8 %copy-start.1 = (bf16[1,16,32,256]{3,2,1,0:T(8,128)(2,1)S(1)}, bf16[1,16,32,256]{3,2,1,0:T(8,128)(2,1)}, u32[]{:S(2)}) copy-start(bf16[1,16,32,256]{3,2,1,0:T(8,128)(2,1)} %get-tuple-element.21) | copy-start | bytes 786436
  81.0 1.0 %copy-start = (bf16[1,16,32,256]{3,2,1,0:T(8,128)(2,1)S(1)}, bf16[1,16,32,256]{3,2,1,0:T(8,128)(2,1)}, u32[]{:S(2)}) copy-start(bf16[1,16,32,256]{3,2,1,0:T(8,128)(2,1)} %get-tuple-element.22) | copy-start | bytes 786436
  82.1 0.7 copy-start.4
  82.1 1.3 %copy-start.3 = (f32[64,192]{1,0:T(8,128)S(1)}, f32[64,192]{1,0:T(8,128)}, u32[]{:S(2)}) copy-start(f32[64,192]{1,0:T(8,128)} %get-tuple-element.26) | copy-start | bytes 147460
  82.1 2.0 %copy-start.2 = (f32[192,256]{1,0:T(8,128)S(1)}, f32[192,256]{1,0:T(8,128)}, u32[]{:S(2)}) copy-start(f32[192,256]{1,0:T(8,128)} %get-tuple-element.27) | copy-start | bytes 589828

commit v3 on v2

--- a/solution.py
+++ b/solution.py
@@ -18,6 +18,9 @@
 C = 256
 S = 192
 PW = 72
+EXPAND_ROWS = 10
+GRAD_ROWS = 18
+UNROLL = 4
 NT_DIMS = (((1,), (1,)), ((), ()))
 TN_DIMS = (((0,), (0,)), ((), ()))
 
@@ -48,7 +51,7 @@
 
 def fused(rows_n, ch_n, scale, x_in, we_ref, tap_ref, se1_ref, se2_ref, wp_ref, c_in,
           out_ref, din_ref, dwe_ref, dk_ref, dse1_ref, dse2_ref, dwp_ref,
-          xsib, csib, rowsend, rowbuf, colsend, colbuf, wesend, webuf, wpbuf, sesend, sebuf, tapsend, tapbuf,
+          xsib, csib, rowsend, rowbuf, colsend, colbuf, webuf, wpbuf, sesend, sebuf, tapsend, tapbuf,
           xf, cf, xs, cs, xnat, cnat, a1, s1, gh, s2, act2, ge, ktile, gacc, dkacc,
           vbuf, zv, xv, cv, gs, ysend, yrecv, zsend, zrecv, xrecv, fsend, frecv,
           dksend, dkyr, dkzr, dkxs, dkxr, dkzs, posend, porecv,
@@ -136,9 +139,8 @@
     colsend[2 * H:3 * H] = jnp.dot(pick, c_ref[...].reshape(H * W, C), preferred_element_type=F32).astype(BF16)
 
     eye = (lax.broadcasted_iota(jnp.int32, (S, S), 0) == lax.broadcasted_iota(jnp.int32, (S, S), 1)).astype(F32).astype(BF16)
-    wesend[...] = lax.dot_general(eye, we_ref[...], NT_DIMS, preferred_element_type=F32).astype(BF16)
-    se2_t = lax.dot_general(eye, se2_ref[...], NT_DIMS, preferred_element_type=F32)
-    sesend[...] = jnp.concatenate([se1_ref[...].astype(F32), se2_t], axis=1).astype(BF16)
+    se_t = jnp.concatenate([se1_ref[...], se2_ref[...]], axis=0)
+    sesend[...] = lax.dot_general(eye, se_t, NT_DIMS, preferred_element_type=F32).astype(BF16)
     tap_rows = jnp.concatenate([tap_ref[...].astype(F32), jnp.zeros((7, S), F32)], axis=0)
     tapsend[...] = jnp.concatenate([tap_rows, jnp.zeros((16, 256 - S), F32)], axis=1).astype(BF16)
 
@@ -163,16 +165,16 @@
     sib_copies[0].start()
     for sent, _ in row_copies + col_copies:
         sent.start()
-    to_y([near], 0, lambda p: wesend, webuf, we_s, we_r)
+    to_y([near], 0, lambda p: we_ref, webuf, we_s, we_r)
     spread(yn, my, at_y, lambda p: tapsend, tapbuf, tap_s, tap_r)
     sib_copies[1].start()
-    to_y(far, 1, lambda p: wesend, webuf, we_s, we_r)
+    to_y(far, 1, lambda p: we_ref, webuf, we_s, we_r)
     to_y([near] + far, 0, lambda p: wp_ref, wpbuf, wp_s, wp_r)
     spread(yn, my, at_y, lambda p: sesend, sebuf.at[mc], se_s, se_r)
     relay = copy(sebuf.at[mc], sebuf.at[mc], rel_s.at[0], rel_r.at[mc], sib)
     relayed = copy(sebuf.at[mc], sebuf.at[oc], rel_s.at[0], rel_r.at[oc], sib)
 
-    webuf[my] = wesend[...]
+    webuf[my] = we_ref[...]
     wpbuf[my] = wp_ref[...]
     tapbuf[my] = tapsend[...]
     sebuf[mc, my] = sesend[...]
@@ -226,24 +228,26 @@
     wide = jnp.concatenate([tapbuf[q].astype(F32)[:, 0:S] for q in range(yn)], axis=1)
     for t in range(nt):
         ktile[t] = wide[:, 128 * t:128 * t + 128]
-    from_y([near], 0, lambda p: wesend, webuf, we_s, we_r)
+    from_y([near], 0, lambda p: we_ref, webuf, we_s, we_r)
 
     for b in range(pairs):
         pair = lax.rem(pair_mine + b, pairs)
         if b == 1:
-            from_y(far, 1, lambda p: wesend, webuf, we_s, we_r)
+            from_y(far, 1, lambda p: we_ref, webuf, we_s, we_r)
         w_exp = webuf[pl.ds(pair * 2, 2)].reshape(2 * S, C)
 
-        @pl.loop(0, (H + 4) // 2)
+        @pl.loop(0, (H + 4) // EXPAND_ROWS)
         def _(i):
-            at = pl.ds(pl.multiple_of(i * 2 * PW, 2 * PW), 2 * PW)
+            step = EXPAND_ROWS * PW
+            at = pl.ds(pl.multiple_of(i * step, step), step)
             pre = lax.dot_general(xs[at], w_exp, NT_DIMS, preferred_element_type=F32)
             sig = sigm(pre)
             act = pre * sig
             slope = sig * (1.0 + (pre - act))
             for t in range(3):
-                a1[pair * 3 + t, pl.ds(i * 2, 2)] = act[:, 128 * t:128 * t + 128].reshape(2, PW, 128)
-                s1[pair * 3 + t, pl.ds(i * 2, 2)] = slope[:, 128 * t:128 * t + 128].reshape(2, PW, 128)
+                there = pl.ds(i * EXPAND_ROWS, EXPAND_ROWS)
+                a1[pair * 3 + t, there] = act[:, 128 * t:128 * t + 128].reshape(EXPAND_ROWS, PW, 128)
+                s1[pair * 3 + t, there] = slope[:, 128 * t:128 * t + 128].reshape(EXPAND_ROWS, PW, 128)
 
         @pl.loop(0, 3)
         def _(t3):
@@ -267,7 +271,7 @@
 
             one_row(0)
             one_row(H + 1)
-            pool = lax.fori_loop(1, H + 1, center, jnp.zeros((8, 128), F32))
+            pool = lax.fori_loop(1, H + 1, center, jnp.zeros((8, 128), F32), unroll=UNROLL)
             vbuf[pl.ds(t, 1)] = jnp.sum(pool, axis=0, keepdims=True)
 
     sib_copies[1].wait()
@@ -348,12 +352,13 @@
     def hidden_grad(pair):
         w_pro = wpbuf[2 * pair:2 * pair + 2].reshape(2 * S, C)
 
-        @pl.loop(0, (H + 2) // 2)
+        @pl.loop(0, (H + 2) // GRAD_ROWS)
         def _(i):
-            at = pl.ds(pl.multiple_of(i * 2 * PW, 2 * PW), 2 * PW)
+            step = GRAD_ROWS * PW
+            at = pl.ds(pl.multiple_of(i * step, step), step)
             back = lax.dot_general(cs[at], w_pro, NT_DIMS, preferred_element_type=F32)
             for t in range(3):
-                gh[pair * 3 + t, pl.ds(i * 2, 2)] = back[:, 128 * t:128 * t + 128].reshape(2, PW, 128)
+                gh[pair * 3 + t, pl.ds(i * GRAD_ROWS, GRAD_ROWS)] = back[:, 128 * t:128 * t + 128].reshape(GRAD_ROWS, PW, 128)
 
     gathered(zn, mz, at_z, lambda p: vbuf, zv, vz_s, vz_r)
     xv[mx] = jnp.sum(zv[...], axis=0)
@@ -443,12 +448,12 @@
             gate_t = gs[0, pl.ds(t, 1)]
             pool_t = gs[1, pl.ds(t, 1)]
 
-            @pl.loop(0, H + 2)
+            @pl.loop(0, H + 2, unroll=2)
             def _(i):
                 keep = jnp.where(((i > 0) | top_ok) & ((i < H + 1) | low_ok), 1.0, 0.0)
                 gh[t, i] = (gh[t, i] * gate_t + pool_t) * s2[t, i] * (inside * keep)
 
-            @pl.loop(0, H)
+            @pl.loop(0, H, unroll=UNROLL)
             def _(i):
                 rows = [gh[t, i + r] for r in range(3)]
                 parts = [taps[c] * rows[2] + taps[3 + c] * rows[1] + taps[6 + c] * rows[0] for c in range(3)]
@@ -482,7 +487,7 @@
                     fresh.append(sums[3 * r + c] + jnp.sum((moved[c] * act).reshape(9, 8, 128), axis=0))
             return tuple(fresh)
 
-        sums = lax.fori_loop(0, H, center, (jnp.zeros((8, 128), F32),) * 9)
+        sums = lax.fori_loop(0, H, center, (jnp.zeros((8, 128), F32),) * 9, unroll=UNROLL)
         dkacc[t] = jnp.concatenate(
             [jnp.sum(part, axis=0, keepdims=True) for part in sums] + [jnp.zeros((7, 128), F32)], axis=0)
 
@@ -516,8 +521,8 @@
     send_back(1)
 
     own_gate = shard_of(gate)
-    lefts, rights = pairs3(shard_of(own(pooled)), grad_squeeze * scale)
-    dse1_ref[...] = lax.dot_general(lefts, rights, TN_DIMS, preferred_element_type=F32)[:, 0:64]
+    lefts, rights = pairs3(grad_squeeze * scale, shard_of(own(pooled)))
+    dse1_ref[...] = lax.dot_general(lefts, rights, TN_DIMS, preferred_element_type=F32)[0:64]
     lefts, rights = pairs3(squeeze_act, shard_of(own(excite)) * scale)
     dse2_ref[...] = lax.dot_general(lefts, rights, TN_DIMS, preferred_element_type=F32)[0:64]
     gate_wide = lax.dot_general(split3(own_gate * scale), ones, TN_DIMS, preferred_element_type=F32)
@@ -527,8 +532,16 @@
     gathered(xn, mx, at_x, lambda p: dkxs, dkxr, kx_s, kx_r)
     dk_ref[...] = summed(dkxr)[0:9, 0:S] * scale
     whole(1, gacc.at[S:2 * S])
-    turned = lax.dot_general(gacc[S:2 * S].astype(BF16), eye, TN_DIMS, preferred_element_type=F32)
-    dwe_ref[...] = turned * scale
+    dwe_ref[...] = gacc[S:2 * S] * scale
+
+
+def settle(*refs):
+    count = (len(refs) - 1) // 2
+    moves = [pltpu.make_async_copy(refs[k], refs[count + k], refs[-1].at[k]) for k in range(count)]
+    for move in moves:
+        move.start()
+    for move in moves:
+        move.wait()
 
 
 def per_device(inputs, w_expand, kernel, w_se1, w_se2, w_project, cotangent):
@@ -544,7 +557,7 @@
         vmem((H, W, C), BF16), vmem((H, W, C), BF16),
         vmem((2, 3 * W, C), BF16), vmem((2, 2, 3 * W, C), BF16),
         vmem((3 * H, C), BF16), vmem((2, 3, 3 * H, C), BF16),
-        vmem((S, C), BF16), vmem((yn, S, C), BF16), vmem((yn, S, C), BF16),
+        vmem((yn, S, C), BF16), vmem((yn, S, C), BF16),
         vmem((S, 128), BF16), vmem((2, yn, S, 128), BF16),
         vmem((16, 256), BF16), vmem((yn, 16, 256), BF16),
         vmem((H + 4, PW, C), F32), vmem((H + 2, PW, C), F32),
@@ -571,19 +584,29 @@
         dma((2,)), dma((2,)),
     ]
     in_vmem = pl.BlockSpec(memory_space=pltpu.VMEM)
-    return pl.pallas_call(
+    shapes = (
+        jax.ShapeDtypeStruct((1, H, W, C), BF16), jax.ShapeDtypeStruct((1, H, W, C), BF16),
+        jax.ShapeDtypeStruct((S, C), F32), jax.ShapeDtypeStruct((9, S), F32),
+        jax.ShapeDtypeStruct((64, S), F32), jax.ShapeDtypeStruct((64, S), F32),
+        jax.ShapeDtypeStruct((S, C), F32))
+    results = pl.pallas_call(
         functools.partial(fused, rows_n, ch_n, grad_scale),
-        out_shape=(
-            jax.ShapeDtypeStruct((1, H, W, C), BF16), jax.ShapeDtypeStruct((1, H, W, C), BF16),
-            jax.ShapeDtypeStruct((C, S), F32), jax.ShapeDtypeStruct((9, S), F32),
-            jax.ShapeDtypeStruct((S, 64), F32), jax.ShapeDtypeStruct((64, S), F32),
-            jax.ShapeDtypeStruct((S, C), F32)),
+        out_shape=shapes,
         in_specs=[in_vmem] * 7,
         out_specs=(in_vmem,) * 7,
         scratch_shapes=scratch,
         compiler_params=pltpu.CompilerParams(
             collective_id=0, has_side_effects=True, vmem_limit_bytes=56 * 1024 * 1024),
-    )(inputs, w_expand, kernel, w_se1, w_se2, w_project, cotangent)
+    )(inputs, w_expand.T, kernel, w_se1.T, w_se2, w_project, cotangent)
+    anywhere = pl.BlockSpec(memory_space=pl.ANY)
+    output, d_input, d_expand_t, d_taps, d_se1_t, d_se2, d_project = pl.pallas_call(
+        settle,
+        out_shape=shapes,
+        in_specs=[anywhere] * 7,
+        out_specs=(anywhere,) * 7,
+        scratch_shapes=[dma((7,))],
+    )(*results)
+    return output, d_input, d_expand_t.T, d_taps, d_se1_t.T, d_se2, d_project
 
 
 def solution(mesh):

time: 85 us -> 103 us (1.21)
  Pallas kernels: 73.8 us -> 102 us
  local copies, waits for them, and re-layouts: 10.2 us -> 0 us
    pallas_call x0 -> x1, Pallas kernels: none -> 33.4 us  [per_device(): pl.pallas_call(settle, out_shape=shapes, in_specs=[anywhere] * 7, out_spe...]
    unnamed x17 -> x0, local copies, waits for them, and re-layouts: 6.81 us -> none
    pallas_call x1, Pallas kernels: 73.8 us -> 68.7 us  [per_device(): pl.pallas_call(functools.partial(fused, rows_n, ch_n, grad_scale), out_sh...]
    pallas_call x2 -> x0, local copies, waits for them, and re-layouts: 3.39 us -> none  [per_device(): pl.pallas_call(functools.partial(fused, rows_n, ch_n, grad_scale), out_sh...]
where the time goes in v3:
time: 103 us
  Pallas kernels  102 us (99%)
    pallas_call x1, Pallas kernels, per_device(): pl.pallas_call(functools.partial(fused, rows_n, ch_n, grad_scale), out_sh...  68.7 us
    pallas_call x1, Pallas kernels, per_device(): pl.pallas_call(settle, out_shape=shapes, in_specs=[anywhere] * 7, out_spe...  33.4 us

profile of v3, /device:TPU:8, one launch (start us, length us, event | category | flops | bytes accessed | tf_op | source)
XLA Modules:
  0.0 102.8 jit_solution(6062700778104782759)
XLA Ops:
  0.6 68.7 %shard_map.126 = (bf16[1,16,32,256]{3,2,1,0:T(8,128)(2,1)}, bf16[1,16,32,256]{3,2,1,0:T(8,128)(2,1)}, f32[192,256]{1,0:T(8,128)}, f32[9,192]{1,0:T(8,128)}, f32[...) custom-call(bf16[1,16,32,256]{3,2,1,0:T(8,128)(2,1)} %x_in.1, bf16[192,256]{1,0:T(8,128)(2,1)} %bitcast.4, ...), custom_call_target="tpu_custom_call" | custom-call | tf_op jit(solution)/shard_map/pallas_call | solution.py:592
  69.4 33.4 %shard_map.127 = (bf16[1,16,32,256]{3,2,1,0:T(8,128)(2,1)}, bf16[1,16,32,256]{3,2,1,0:T(8,128)(2,1)}, f32[192,256]{1,0:T(8,128)}, f32[9,192]{1,0:T(8,128)}, f32[...) custom-call(bf16[1,16,32,256]{3,2,1,0:T(8,128)(2,1)} %get-tuple-element.21.refs_0_, ...), custom_call_target="tpu_custom_call" | custom-call | tf_op jit(solution)/shard_map/pallas_call | solution.py:602

commit v4 on v3

--- a/solution.py
+++ b/solution.py
@@ -52,7 +52,7 @@
 def fused(rows_n, ch_n, scale, x_in, we_ref, tap_ref, se1_ref, se2_ref, wp_ref, c_in,
           out_ref, din_ref, dwe_ref, dk_ref, dse1_ref, dse2_ref, dwp_ref,
           xsib, csib, rowsend, rowbuf, colsend, colbuf, webuf, wpbuf, sesend, sebuf, tapsend, tapbuf,
-          xf, cf, xs, cs, xnat, cnat, a1, s1, gh, s2, act2, ge, ktile, gacc, dkacc,
+          xf, cf, xs, cs, xnat, cnat, a1, s1, gh, s2, ca, cb, act2, ge, ktile, gacc, dkacc,
           vbuf, zv, xv, cv, gs, ysend, yrecv, zsend, zrecv, xrecv, fsend, frecv,
           dksend, dkyr, dkzr, dkxs, dkxr, dkzs, posend, porecv,
           sib_s, sib_r, row_s, row_r, col_s, col_r, we_s, we_r, wp_s, wp_r, se_s, se_r, rel_s, rel_r, tap_s, tap_r,
@@ -360,15 +360,44 @@
             for t in range(3):
                 gh[pair * 3 + t, pl.ds(i * GRAD_ROWS, GRAD_ROWS)] = back[:, 128 * t:128 * t + 128].reshape(GRAD_ROWS, PW, 128)
 
+    place = lax.broadcasted_iota(jnp.int32, (PW, 128), 0)
+    off_left = jnp.where(left_ok, PW, PW - 1)
+    off_right = jnp.where(right_ok, 0, 1)
+    inside = jnp.where((place < 64) | ((place == 64) & (off_right == 0)) | ((place == PW - 1) & (off_left == PW)), 1.0, 0.0)
+
+    def depth_back(pair):
+        @pl.loop(0, 3)
+        def _(t3):
+            t = pair * 3 + t3
+            taps = [ktile[t, k:k + 1] for k in range(9)]
+
+            @pl.loop(0, H + 2, unroll=2)
+            def _(i):
+                keep = jnp.where(((i > 0) | top_ok) & ((i < H + 1) | low_ok), 1.0, 0.0)
+                slope = s2[t, i] * (inside * keep)
+                s2[t, i] = slope
+                gh[t, i] = gh[t, i] * slope
+
+            @pl.loop(0, H, unroll=UNROLL)
+            def _(i):
+                first_slope = s1[t, i + 2, 0:64]
+                for source, into in ((gh, ca), (s2, cb)):
+                    rows = [source[t, i + r] for r in range(3)]
+                    parts = [taps[c] * rows[2] + taps[3 + c] * rows[1] + taps[6 + c] * rows[0] for c in range(3)]
+                    grad = parts[1] + pltpu.roll(parts[0], PW - 1, 0) + pltpu.roll(parts[2], 1, 0)
+                    into[t, i] = grad[0:64] * first_slope
+
+    for pair in range(pairs):
+        hidden_grad(pair)
     gathered(zn, mz, at_z, lambda p: vbuf, zv, vz_s, vz_r)
     xv[mx] = jnp.sum(zv[...], axis=0)
     spread(xn, mx, at_x, lambda p: xv.at[mx], xv, vx_s, vx_r)
-    hidden_grad(0)
+    depth_back(0)
     gathered(xn, mx, at_x, lambda p: xv.at[mx], xv, vx_s, vx_r)
     cv[ch] = jnp.sum(xv[...], axis=0)
     spread(ch_n, ch, at_ch, lambda p: cv.at[ch], cv, vc_s, vc_r)
     for pair in range(1, pairs):
-        hidden_grad(pair)
+        depth_back(pair)
     gathered(ch_n, ch, at_ch, lambda p: cv.at[ch], cv, vc_s, vc_r)
     relayed.wait()
 
@@ -431,11 +460,6 @@
         copy(posend.at[k], porecv.at[k], po_s.at[k], po_r.at[k], sib).wait()
         into[0] = (base[...].astype(F32) + (total[...] + porecv[k].astype(F32))).astype(BF16)
 
-    place = lax.broadcasted_iota(jnp.int32, (PW, 128), 0)
-    off_left = jnp.where(left_ok, PW, PW - 1)
-    off_right = jnp.where(right_ok, 0, 1)
-    inside = jnp.where((place < 64) | ((place == 64) & (off_right == 0)) | ((place == PW - 1) & (off_left == PW)), 1.0, 0.0)
-
     x_flat = xnat[...].reshape(H * 64, C)
     for b in range(pairs):
         pair = lax.rem(pair_mine + 1 + b, pairs)
@@ -444,21 +468,12 @@
         def _(t3):
             t = pair * 3 + t3
             lanes = pl.ds(pl.multiple_of(t * 128, 128), 128)
-            taps = [ktile[t, k:k + 1] for k in range(9)]
             gate_t = gs[0, pl.ds(t, 1)]
             pool_t = gs[1, pl.ds(t, 1)]
 
-            @pl.loop(0, H + 2, unroll=2)
-            def _(i):
-                keep = jnp.where(((i > 0) | top_ok) & ((i < H + 1) | low_ok), 1.0, 0.0)
-                gh[t, i] = (gh[t, i] * gate_t + pool_t) * s2[t, i] * (inside * keep)
-
             @pl.loop(0, H, unroll=UNROLL)
             def _(i):
-                rows = [gh[t, i + r] for r in range(3)]
-                parts = [taps[c] * rows[2] + taps[3 + c] * rows[1] + taps[6 + c] * rows[0] for c in range(3)]
-                grad = parts[1] + pltpu.roll(parts[0], PW - 1, 0) + pltpu.roll(parts[2], 1, 0)
-                ge[i, :, lanes] = (grad[0:64] * s1[t, i + 2, 0:64]).astype(BF16)
+                ge[i, :, lanes] = (ca[t, i] * gate_t + cb[t, i] * pool_t).astype(BF16)
 
         lanes3 = pl.ds(pl.multiple_of(pair * 384, 384), 384)
         rows = lax.dot_general(ge[:, :, lanes3].reshape(H * 64, 384), x_flat, TN_DIMS, preferred_element_type=F32)
@@ -477,8 +492,12 @@
 
     @pl.loop(0, nt)
     def _(t):
+        gate_t = gs[0, pl.ds(t, 1)]
+        pool_t = gs[1, pl.ds(t, 1)]
+
         def center(i, sums):
-            here = jnp.concatenate([gh[t, i + 1, 0:64], jnp.zeros((8, 128), F32)], axis=0)
+            grad = gh[t, i + 1, 0:64] * gate_t + s2[t, i + 1, 0:64] * pool_t
+            here = jnp.concatenate([grad, jnp.zeros((8, 128), F32)], axis=0)
             moved = [pltpu.roll(here, PW - 1, 0), here, pltpu.roll(here, 1, 0)]
             fresh = []
             for r in range(3):
@@ -565,6 +584,7 @@
         vmem((H, 64, C), BF16), vmem((H, 64, C), BF16),
         vmem((nt, H + 4, PW, 128), F32), vmem((nt, H + 4, PW, 128), F32),
         vmem((nt, H + 2, PW, 128), F32), vmem((nt, H + 2, PW, 128), F32),
+        vmem((nt, H, 64, 128), F32), vmem((nt, H, 64, 128), F32),
         vmem((H, 64, ce), BF16), vmem((H, 64, ce), BF16),
         vmem((nt, 16, 128), F32), vmem((ce, C), F32), vmem((nt, 16, 128), F32),
         vmem((16, 128), F32), vmem((zn, 16, 128), F32), vmem((xn, 16, 128), F32), vmem((ch_n, 16, 128), F32),
@@ -603,7 +623,7 @@
         settle,
         out_shape=shapes,
         in_specs=[anywhere] * 7,
-        out_specs=(anywhere,) * 7,
+        out_specs=(in_vmem,) * 7,
         scratch_shapes=[dma((7,))],
     )(*results)
     return output, d_input, d_expand_t.T, d_taps, d_se1_t.T, d_se2, d_project

time: 103 us -> 71.9 us (0.70)
  Pallas kernels: 102 us -> 71.2 us
    pallas_call x1, Pallas kernels: 33.4 us -> 2.23 us  [per_device(): pl.pallas_call(settle, out_shape=shapes, in_specs=[anywhere] * 7, out_spe...]
where the time goes in v4:
time: 71.9 us; the launch traced here: 71.8 us
  Pallas kernels  71.2 us (99%)
    pallas_call x1, Pallas kernels, per_device(): pl.pallas_call(functools.partial(fused, rows_n, ch_n, grad_scale), out_sh...  68.9 us
    pallas_call x1, Pallas kernels, per_device(): pl.pallas_call(settle, out_shape=shapes, in_specs=[anywhere] * 7, out_spe...  2.23 us

profile of v4, /device:TPU:8, one launch (start us, length us, event | category | flops | bytes accessed | tf_op | source)
XLA Modules:
  0.0 71.8 jit_solution(13843187735001990873)
XLA Ops:
  0.6 68.9 %shard_map.126 = (bf16[1,16,32,256]{3,2,1,0:T(8,128)(2,1)}, bf16[1,16,32,256]{3,2,1,0:T(8,128)(2,1)}, f32[192,256]{1,0:T(8,128)}, f32[9,192]{1,0:T(8,128)}, f32[...) custom-call(bf16[1,16,32,256]{3,2,1,0:T(8,128)(2,1)} %x_in.1, bf16[192,256]{1,0:T(8,128)(2,1)} %bitcast.4, ...), custom_call_target="tpu_custom_call" | custom-call | tf_op jit(solution)/shard_map/pallas_call | solution.py:612
  69.6 2.2 %shard_map.127 = (bf16[1,16,32,256]{3,2,1,0:T(8,128)(2,1)}, bf16[1,16,32,256]{3,2,1,0:T(8,128)(2,1)}, f32[192,256]{1,0:T(8,128)}, f32[9,192]{1,0:T(8,128)}, f32[...) custom-call(bf16[1,16,32,256]{3,2,1,0:T(8,128)(2,1)} %get-tuple-element.21.refs_0_, ...), custom_call_target="tpu_custom_call" | custom-call | tf_op jit(solution)/shard_map/pallas_call | solution.py:622

commit v5 on v4

--- a/solution.py
+++ b/solution.py
@@ -49,16 +49,15 @@
     return lefts, rights
 
 
-def fused(rows_n, ch_n, scale, x_in, we_ref, tap_ref, se1_ref, se2_ref, wp_ref, c_in,
+def fused(rows_n, ch_n, scale, x_in, we_in, tap_in, se1_in, se2_in, wp_in, c_in,
           out_ref, din_ref, dwe_ref, dk_ref, dse1_ref, dse2_ref, dwp_ref,
-          xsib, csib, rowsend, rowbuf, colsend, colbuf, webuf, wpbuf, sesend, sebuf, tapsend, tapbuf,
+          x_ref, we_ref, tap_ref, se1_ref, se2_ref, wp_ref, c_ref, xsib, csib, rowsend, rowbuf, colsend, colbuf, webuf, wpbuf, sesend, sebuf, tapsend, tapbuf,
           xf, cf, xs, cs, xnat, cnat, a1, s1, gh, s2, ca, cb, act2, ge, ktile, gacc, dkacc,
           vbuf, zv, xv, cv, gs, ysend, yrecv, zsend, zrecv, xrecv, fsend, frecv,
           dksend, dkyr, dkzr, dkxs, dkxr, dkzs, posend, porecv,
-          sib_s, sib_r, row_s, row_r, col_s, col_r, we_s, we_r, wp_s, wp_r, se_s, se_r, rel_s, rel_r, tap_s, tap_r,
+          load_s, sib_s, sib_r, row_s, row_r, col_s, col_r, we_s, we_r, wp_s, wp_r, se_s, se_r, rel_s, rel_r, tap_s, tap_r,
           vz_s, vz_r, vx_s, vx_r, vc_s, vc_r, gy_s, gy_r, gz_s, gz_r, gx_s, gx_r, gf_s, gf_r,
           ky_s, ky_r, kz_s, kz_r, kx_s, kx_r, po_s, po_r):
-    x_ref, c_ref = x_in.at[0], c_in.at[0]
     zn = CHIPS_Z if rows_n % CHIPS_Z == 0 else 2
     xn = rows_n // zn
     yn = ch_n // 2
@@ -124,6 +123,14 @@
     partners += [(dev_row(dr), dev_y(dy) * 2 + core) for dr in (-1, 0, 1) for dy in (-1, 1) for core in (0, 1)]
     for where in partners:
         pl.semaphore_signal(barrier, inc=1, device_id=where, device_id_type=MESH)
+
+    arrays = ((x_in.at[0], x_ref), (c_in.at[0], c_ref), (we_in, we_ref), (tap_in, tap_ref), (se1_in, se1_ref),
+              (se2_in, se2_ref), (wp_in, wp_ref))
+    loads = [pltpu.make_async_copy(source, into, load_s.at[k]) for k, (source, into) in enumerate(arrays)]
+    for load in loads:
+        load.start()
+    for load in loads:
+        load.wait()
 
     for d, (lo, edge) in enumerate(((0, 0), (H - 2, H - 1))):
         rowsend[d, 0:2 * W] = x_ref[lo:lo + 2].reshape(2 * W, C)
@@ -396,6 +403,7 @@
     gathered(xn, mx, at_x, lambda p: xv.at[mx], xv, vx_s, vx_r)
     cv[ch] = jnp.sum(xv[...], axis=0)
     spread(ch_n, ch, at_ch, lambda p: cv.at[ch], cv, vc_s, vc_r)
+    send_z(0)
     for pair in range(1, pairs):
         depth_back(pair)
     gathered(ch_n, ch, at_ch, lambda p: cv.at[ch], cv, vc_s, vc_r)
@@ -439,7 +447,7 @@
     for t in range(nt):
         gs[0, t:t + 1] = gate[:, 128 * t:128 * t + 128]
         gs[1, t:t + 1] = grad_pool[:, 128 * t:128 * t + 128]
-    send_z(0)
+    send_x(0)
 
     def shard_of(rows):
         part = rows[:, 0:S]
@@ -480,14 +488,11 @@
         ysend[1, pl.ds(pair * 2, 2)] = rows.reshape(2, S, C).astype(BF16)
         if b < pairs - 1:
             to_y(far, 1, lambda p: ysend.at[1, p], yrecv.at[1], gy_s.at[1], gy_r.at[1])
-            send_x(0)
         else:
             to_y([near], 0, lambda p: ysend.at[1, p], yrecv.at[1], gy_s.at[1], gy_r.at[1])
             yrecv[1, my] = ysend[1, my]
 
     project(ge, 1, webuf[...].reshape(ce, C), cf.at[0:H, 0:W])
-    if pairs == 1:
-        send_x(0)
     send_back(0)
 
     @pl.loop(0, nt)
@@ -573,6 +578,8 @@
     grad_scale = 1.0 / math.sqrt(rows_n * H * ch_n * W)
     vmem, dma = pltpu.VMEM, pltpu.SemaphoreType.DMA
     scratch = [
+        vmem((H, W, C), BF16), vmem((S, C), BF16), vmem((9, S), BF16), vmem((64, S), BF16), vmem((64, S), BF16),
+        vmem((S, C), BF16), vmem((H, W, C), BF16),
         vmem((H, W, C), BF16), vmem((H, W, C), BF16),
         vmem((2, 3 * W, C), BF16), vmem((2, 2, 3 * W, C), BF16),
         vmem((3 * H, C), BF16), vmem((2, 3, 3 * H, C), BF16),
@@ -595,7 +602,7 @@
         vmem((16, ce), BF16), vmem((yn, 16, ce), BF16),
         vmem((zn, 16, 256), BF16), vmem((16, 256), BF16), vmem((xn, 16, 256), BF16), vmem((16, 256), BF16),
         vmem((2, H, W, C), BF16), vmem((2, H, W, C), BF16),
-        dma((2,)), dma((2,)), dma((2, 2)), dma((2, 2)), dma((3, 2)), dma((2, 3)),
+        dma((7,)), dma((2,)), dma((2,)), dma((2, 2)), dma((2, 2)), dma((3, 2)), dma((2, 3)),
         dma((yn,)), dma((yn,)), dma((yn,)), dma((yn,)),
         dma((yn,)), dma((yn,)), dma((1,)), dma((2,)), dma((yn,)), dma((yn,)),
         dma((zn,)), dma((zn,)), dma((xn,)), dma((xn,)), dma((ch_n,)), dma((ch_n,)),
@@ -603,6 +610,7 @@
         dma((yn,)), dma((yn,)), dma((zn,)), dma((zn,)), dma((xn,)), dma((xn,)),
         dma((2,)), dma((2,)),
     ]
+    anywhere = pl.BlockSpec(memory_space=pl.ANY)
     in_vmem = pl.BlockSpec(memory_space=pltpu.VMEM)
     shapes = (
         jax.ShapeDtypeStruct((1, H, W, C), BF16), jax.ShapeDtypeStruct((1, H, W, C), BF16),
@@ -612,13 +620,12 @@
     results = pl.pallas_call(
         functools.partial(fused, rows_n, ch_n, grad_scale),
         out_shape=shapes,
-        in_specs=[in_vmem] * 7,
+        in_specs=[anywhere] * 7,
         out_specs=(in_vmem,) * 7,
         scratch_shapes=scratch,
         compiler_params=pltpu.CompilerParams(
             collective_id=0, has_side_effects=True, vmem_limit_bytes=56 * 1024 * 1024),
     )(inputs, w_expand.T, kernel, w_se1.T, w_se2, w_project, cotangent)
-    anywhere = pl.BlockSpec(memory_space=pl.ANY)
     output, d_input, d_expand_t, d_taps, d_se1_t, d_se2, d_project = pl.pallas_call(
         settle,
         out_shape=shapes,

time: 71.9 us -> 66.9 us (0.930)
  Pallas kernels: 71.2 us -> 66.1 us
    pallas_call x1, Pallas kernels: 68.9 us -> 63.9 us  [per_device(): pl.pallas_call(functools.partial(fused, rows_n, ch_n, grad_scale), out_sh...]
where the time goes in v5:
time: 66.9 us; the launch traced here: 66.8 us
  Pallas kernels  66.1 us (99%)
    pallas_call x1, Pallas kernels, per_device(): pl.pallas_call(functools.partial(fused, rows_n, ch_n, grad_scale), out_sh...  63.9 us
    pallas_call x1, Pallas kernels, per_device(): pl.pallas_call(settle, out_shape=shapes, in_specs=[anywhere] * 7, out_spe...  2.23 us

profile of v5, /device:TPU:8, one launch (start us, length us, event | category | flops | bytes accessed | tf_op | source)
XLA Modules:
  0.0 66.8 jit_solution(3283109798579778230)
XLA Ops:
  0.6 63.9 %shard_map.126 = (bf16[1,16,32,256]{3,2,1,0:T(8,128)(2,1)}, bf16[1,16,32,256]{3,2,1,0:T(8,128)(2,1)}, f32[192,256]{1,0:T(8,128)}, f32[9,192]{1,0:T(8,128)}, f32[...) custom-call(bf16[1,16,32,256]{3,2,1,0:T(8,128)(2,1)} %x_in.1, bf16[192,256]{1,0:T(8,128)(2,1)} %bitcast.4, ...), custom_call_target="tpu_custom_call" | custom-call | tf_op jit(solution)/shard_map/pallas_call | solution.py:620
  64.5 2.2 %shard_map.127 = (bf16[1,16,32,256]{3,2,1,0:T(8,128)(2,1)}, bf16[1,16,32,256]{3,2,1,0:T(8,128)(2,1)}, f32[192,256]{1,0:T(8,128)}, f32[9,192]{1,0:T(8,128)}, f32[...) custom-call(bf16[1,16,32,256]{3,2,1,0:T(8,128)(2,1)} %get-tuple-element.21.refs_0_, ...), custom_call_target="tpu_custom_call" | custom-call | tf_op jit(solution)/shard_map/pallas_call | solution.py:629

commit v6 on v5

--- a/solution.py
+++ b/solution.py
@@ -20,7 +20,7 @@
 PW = 72
 EXPAND_ROWS = 10
 GRAD_ROWS = 18
-UNROLL = 4
+UNROLL = 8
 NT_DIMS = (((1,), (1,)), ((), ()))
 TN_DIMS = (((0,), (0,)), ((), ()))
 
@@ -493,8 +493,6 @@
             yrecv[1, my] = ysend[1, my]
 
     project(ge, 1, webuf[...].reshape(ce, C), cf.at[0:H, 0:W])
-    send_back(0)
-
     @pl.loop(0, nt)
     def _(t):
         gate_t = gs[0, pl.ds(t, 1)]
@@ -537,6 +535,7 @@
     spread(zn, mz, at_z, lambda p: dkzs, dkzr, kz_s, kz_r)
     dkzr[mz] = dkzs[...]
     send_x(1)
+    send_back(0)
     projected(1, c_ref, cf.at[0:H, 0:W], din_ref)
     gathered(zn, mz, at_z, lambda p: dkzs, dkzr, kz_s, kz_r)
     dkxs[...] = summed(dkzr).astype(BF16)

time: 66.9 us -> 66.2 us (0.990)
  Pallas kernels: 66.1 us -> 64.9 us
    pallas_call x1, Pallas kernels: 63.9 us -> 62.7 us  [per_device(): pl.pallas_call(functools.partial(fused, rows_n, ch_n, grad_scale), out_sh...]
where the time goes in v6:
time: 66.2 us; the launch traced here: 65.6 us
  Pallas kernels  64.9 us (98%)
    pallas_call x1, Pallas kernels, per_device(): pl.pallas_call(functools.partial(fused, rows_n, ch_n, grad_scale), out_sh...  62.7 us
    pallas_call x1, Pallas kernels, per_device(): pl.pallas_call(settle, out_shape=shapes, in_specs=[anywhere] * 7, out_spe...  2.23 us

profile of v6, /device:TPU:8, one launch (start us, length us, event | category | flops | bytes accessed | tf_op | source)
XLA Modules:
  0.0 65.6 jit_solution(11375283318317574603)
XLA Ops:
  0.6 62.7 %shard_map.126 = (bf16[1,16,32,256]{3,2,1,0:T(8,128)(2,1)}, bf16[1,16,32,256]{3,2,1,0:T(8,128)(2,1)}, f32[192,256]{1,0:T(8,128)}, f32[9,192]{1,0:T(8,128)}, f32[...) custom-call(bf16[1,16,32,256]{3,2,1,0:T(8,128)(2,1)} %x_in.1, bf16[192,256]{1,0:T(8,128)(2,1)} %bitcast.4, ...), custom_call_target="tpu_custom_call" | custom-call | tf_op jit(solution)/shard_map/pallas_call | solution.py:619
  63.3 2.2 %shard_map.127 = (bf16[1,16,32,256]{3,2,1,0:T(8,128)(2,1)}, bf16[1,16,32,256]{3,2,1,0:T(8,128)(2,1)}, f32[192,256]{1,0:T(8,128)}, f32[9,192]{1,0:T(8,128)}, f32[...) custom-call(bf16[1,16,32,256]{3,2,1,0:T(8,128)(2,1)} %get-tuple-element.21.refs_0_, ...), custom_call_target="tpu_custom_call" | custom-call | tf_op jit(solution)/shard_map/pallas_call | solution.py:628

commit v7 on v6

--- a/solution.py
+++ b/solution.py
@@ -18,7 +18,7 @@
 C = 256
 S = 192
 PW = 72
-EXPAND_ROWS = 10
+EXPAND_ROWS = 20
 GRAD_ROWS = 18
 UNROLL = 8
 NT_DIMS = (((1,), (1,)), ((), ()))
@@ -120,7 +120,7 @@
     partners += [at_z(lax.rem(mz + s, zn)) for s in range(1, zn)]
     partners += [at_x(lax.rem(mx + s, xn)) for s in range(1, xn)]
     partners += [(dev_row(dr), my * 2 + core) for dr in (-1, 1) for core in (0, 1)]
-    partners += [(dev_row(dr), dev_y(dy) * 2 + core) for dr in (-1, 0, 1) for dy in (-1, 1) for core in (0, 1)]
+    partners += [(dev_row(dr), dev_y(dy) * 2 + core) for dr in (-1, 1) for dy in (-1, 1) for core in (0, 1)]
     for where in partners:
         pl.semaphore_signal(barrier, inc=1, device_id=where, device_id_type=MESH)
 

time: 66.2 us -> 65.7 us (level)
  no operation moved by 1% of the time
where the time goes in v7:
time: 65.7 us; the launch traced here: 65.5 us
  Pallas kernels  64.8 us (99%)
    pallas_call x1, Pallas kernels, per_device(): pl.pallas_call(functools.partial(fused, rows_n, ch_n, grad_scale), out_sh...  62.6 us
    pallas_call x1, Pallas kernels, per_device(): pl.pallas_call(settle, out_shape=shapes, in_specs=[anywhere] * 7, out_spe...  2.23 us

profile of v7, /device:TPU:8, one launch (start us, length us, event | category | flops | bytes accessed | tf_op | source)
XLA Modules:
  0.0 65.5 jit_solution(9528113884819816443)
XLA Ops:
  0.6 62.6 %shard_map.126 = (bf16[1,16,32,256]{3,2,1,0:T(8,128)(2,1)}, bf16[1,16,32,256]{3,2,1,0:T(8,128)(2,1)}, f32[192,256]{1,0:T(8,128)}, f32[9,192]{1,0:T(8,128)}, f32[...) custom-call(bf16[1,16,32,256]{3,2,1,0:T(8,128)(2,1)} %x_in.1, bf16[192,256]{1,0:T(8,128)(2,1)} %bitcast.4, ...), custom_call_target="tpu_custom_call" | custom-call | tf_op jit(solution)/shard_map/pallas_call | solution.py:619
  63.3 2.2 %shard_map.127 = (bf16[1,16,32,256]{3,2,1,0:T(8,128)(2,1)}, bf16[1,16,32,256]{3,2,1,0:T(8,128)(2,1)}, f32[192,256]{1,0:T(8,128)}, f32[9,192]{1,0:T(8,128)}, f32[...) custom-call(bf16[1,16,32,256]{3,2,1,0:T(8,128)(2,1)} %get-tuple-element.21.refs_0_, ...), custom_call_target="tpu_custom_call" | custom-call | tf_op jit(solution)/shard_map/pallas_call | solution.py:628
